TPU v7x, 512 devices: a whole 4x8x8 slice. The times are simulated.
512 devices in a mesh: ens: 8 (over x, core), row: 16 (over y_hi, z), col: 4 (over y_lo).
Axes of the slice: x: 4, y: 8 (y_hi: 2, y_lo: 4; y = y_hi * 4 + y_lo), z: 8, core: 2. Of those that a mesh axis runs over, the one named last changes fastest.
Arguments:
- theta: float32 [64, 1024, 1024], P('ens', 'row', 'col'), may hold values from -1.2 to 1.2
- initial: float32 [1024, 1024], P('row', 'col'), may hold values from -6 to 6
- velocity: float32 [2, 1024, 1024], P(None, 'row', 'col'), may hold values from -4 to 4
- sensors: int32 [16, 4, 256], P('row', 'col'), may hold values from 0 to 16383
- target: float32 [16, 4, 256], P('row', 'col'), may hold values from -6 to 6
- noise: float32 [16, 4, 256], P('row', 'col'), may hold values from 0.5 to 5
Outputs:
- theta_new: float32 [64, 1024, 1024], P('ens', 'row', 'col')
- predictions: float32 [64, 16, 4, 256], P('ens', 'row', 'col')
Inputs may be any that keep to these rules, and one draw needn't show every extreme that they name: `sensors`: an entry is r * 256 + c for a cell at row r and column c of the block of 64 x 256 cells of the device with those row and col indices.
All inputs are finite; a program needn't handle non-finite values.
Results may differ from a plain program's by a relative error of at most 0.0003.
Values sent between devices are 32-bit elements; how exact they have to be, the bound alone decides.
A program may use at most 64 MiB of HBM per device.

v0:
```python
import jax
import jax.numpy as jnp
from jax import lax
from jax.sharding import PartitionSpec as P

STEPS = 4


diffuse_rate = 0.07
advect_rate = 0.3


def padded_2(shard, sides, width):
    for axis, dim in sides:
        size, length = (lax.axis_size(axis), shard.shape[dim])
        up = [(i, (i + 1) % size) for i in range(size - 1)]
        down = [(j, i) for i, j in up]
        last = lax.slice_in_dim(shard, length - width, length, axis=dim)
        leading = lax.slice_in_dim(shard, 0, width, axis=dim)
        before = lax.ppermute(last, axis, up)
        after = lax.ppermute(leading, axis, down)
        shard = jnp.concatenate([before, shard, after], axis=dim)
    return shard


def advance(state, kappa, vel_row, vel_col):
    center = state[:, 1:-1, 1:-1]
    kappa_mid = kappa[:, 1:-1, 1:-1]
    upper = state[:, 2:, 1:-1]
    lower = state[:, :-2, 1:-1]
    right_cell = state[:, 1:-1, 2:]
    left_cell = state[:, 1:-1, :-2]
    face_up = 0.5 * (kappa_mid + kappa[:, 2:, 1:-1])
    face_down = 0.5 * (kappa_mid + kappa[:, :-2, 1:-1])
    face_right = 0.5 * (kappa_mid + kappa[:, 1:-1, 2:])
    face_left = 0.5 * (kappa_mid + kappa[:, 1:-1, :-2])
    flux = (
        face_up * (upper - center)
        - face_down * (center - lower)
        + face_right * (right_cell - center)
        - face_left * (center - left_cell)
    )
    transport = vel_row[1:-1, 1:-1] * (upper - lower) + vel_col[1:-1, 1:-1] * (
        right_cell - left_cell
    )
    return center + diffuse_rate * flux - 0.5 * advect_rate * transport


def shards(theta, initial, velocity, sensors, target, noise):
    members_here = theta.shape[0]
    rows_here = theta.shape[1]
    cols_here = theta.shape[2]
    stacked = jnp.concatenate([jnp.exp(theta), initial[None], velocity], axis=0)
    padded = padded_2(stacked, (("row", 1), ("col", 2)), 1)
    kappa_pad = padded[:members_here]
    vel_row = padded[members_here + 1]
    vel_col = padded[members_here + 2]
    start_field = jnp.broadcast_to(padded[members_here], (members_here,) + padded.shape[1:])
    field = advance(start_field, kappa_pad, vel_row, vel_col)
    for step_index in range(1, STEPS):
        framed = padded_2(field, (("row", 1), ("col", 2)), 1)
        field = advance(framed, kappa_pad, vel_row, vel_col)
    flat_field = field.reshape(members_here, rows_here * cols_here)
    predicted = jnp.take(flat_field, sensors.reshape(-1), axis=1)
    everyone = lax.all_gather(predicted, "ens", axis=0, tiled=True)
    mean_obs = jnp.mean(everyone, axis=0)
    anomalies = everyone - mean_obs
    weighted = anomalies / noise.reshape(-1)
    miss = target.reshape(-1) - everyone
    gram_part = jnp.dot(
        weighted, anomalies.T, precision=lax.Precision.HIGHEST, preferred_element_type=jnp.float32
    )
    cross_part = jnp.dot(
        weighted, miss.T, precision=lax.Precision.HIGHEST, preferred_element_type=jnp.float32
    )
    gram, cross = lax.psum((gram_part, cross_part), ("row", "col"))
    members = everyone.shape[0]
    system = jnp.eye(members, dtype=jnp.float32) + gram / (members - 1)
    factor = jnp.linalg.cholesky(system)
    mixing = jax.scipy.linalg.cho_solve((factor, True), cross) / (members - 1)
    own_columns = lax.dynamic_slice_in_dim(
        mixing, lax.axis_index("ens") * members_here, members_here, 1
    )
    theta_new = theta + jnp.einsum(
        "krc,km->mrc",
        lax.all_gather(theta, "ens", axis=0, tiled=True),
        own_columns,
        precision=lax.Precision.HIGHEST,
    )
    return (theta_new, predicted.reshape(members_here, 1, 1, -1))


def solution(mesh):
    in_specs = (
        P("ens", "row", "col"),
        P("row", "col"),
        P(None, "row", "col"),
        P("row", "col", None),
        P("row", "col", None),
        P("row", "col", None),
    )
    out_specs = (P("ens", "row", "col"), P("ens", "row", "col", None))
    return jax.shard_map(shards, mesh=mesh, in_specs=in_specs, out_specs=out_specs, check_vma=False)
```

profile of v0, /device:TPU:288, one launch (start us, length us, event | category | flops | bytes accessed | tf_op | source)
XLA Modules:
  0.0 458.7 jit_solution(12945836915990543586)
XLA Ops:
  11.3 3.4 collective-permute-start
  14.7 3.7 collective-permute-start.1
  21.5 2.6 collective-permute-start.2
  25.4 5.9 %collective-permute-done.2 = f32[11,66,1]{2,1,0:T(8,128)S(1)} collective-permute-done((f32[11,66,1]{2,1,0:T(8,128)S(1)}, f32[11,66,1]{2,1,0:T(8,128)S(1)}, u32[]{:S(2)}, u32[]{:S(2)}) %collective-permute-start.2) | collective-permute-done | bytes 2936 | tf_op jit(solution)/shard_map/ppermute | solution.py:20
  31.2 4.1 collective-permute-done.3
  36.4 4.9 %collective-permute-start.4 = (f32[8,1,256]{2,1,0:T(1,128)S(1)}, f32[8,1,256]{2,1,0:T(1,128)S(1)}, u32[]{:S(2)}, u32[]{:S(2)}) collective-permute-start(f32[8,1,256]{2,1,0:T(1,128)S(1)} %get-tuple-element.29), channel_id=1, source_target_pairs={{4,0},{8,4},{12,8},{16,12},{20,16},{24,20},{28,24},{32,28},{36,32}... | collective-permute-start | bytes 24584 | tf_op jit(solution)/shard_map/ppermute | solution.py:21
  43.3 4.8 %collective-permute-done.5 = f32[8,1,256]{2,1,0:T(1,128)S(1)} collective-permute-done((f32[8,1,256]{2,1,0:T(1,128)S(1)}, f32[8,1,256]{2,1,0:T(1,128)S(1)}, u32[]{:S(2)}, u32[]{:S(2)}) %collective-permute-start.5) | collective-permute-done | bytes 8224 | tf_op jit(solution)/shard_map/ppermute | solution.py:20
  49.6 4.6 collective-permute-start.7
  54.2 2.7 collective-permute-done.6
  61.2 3.9 collective-permute-start.9
  65.1 2.8 collective-permute-done.9
  69.4 5.0 %collective-permute-start.11 = (f32[8,66,1]{2,1,0:T(8,128)S(1)}, f32[8,66,1]{2,1,0:T(8,128)S(1)}, u32[]{:S(2)}, u32[]{:S(2)}) collective-permute-start(f32[8,66,1]{2,1,0:T(8,128)S(1)} %get-tuple-element.22), channel_id=1, source_target_pairs={{0,1},{1,2},{2,3},{4,5},{5,6},{6,7},{8,9},{9,10},{10,11},{12,13},{... | collective-permute-start | bytes 6344 | tf_op jit(solution)/shard_map/ppermute | solution.py:20
  74.5 2.7 collective-permute-done.10
  79.6 5.5 %collective-permute-start.12 = (f32[8,1,256]{2,1,0:T(1,128)S(1)}, f32[8,1,256]{2,1,0:T(1,128)S(1)}, u32[]{:S(2)}, u32[]{:S(2)}) collective-permute-start(f32[8,1,256]{2,1,0:T(1,128)S(1)} %get-tuple-element.25), channel_id=1, source_target_pairs={{4,0},{8,4},{12,8},{16,12},{20,16},{24,20},{28,24},{32,28},{36,32}... | collective-permute-start | bytes 24584 | tf_op jit(solution)/shard_map/ppermute | solution.py:21
  87.0 9.7 %collective-permute-done.13 = f32[8,1,256]{2,1,0:T(1,128)S(1)} collective-permute-done((f32[8,1,256]{2,1,0:T(1,128)S(1)}, f32[8,1,256]{2,1,0:T(1,128)S(1)}, u32[]{:S(2)}, u32[]{:S(2)}) %collective-permute-start.13) | collective-permute-done | bytes 8224 | tf_op jit(solution)/shard_map/ppermute | solution.py:20
  98.9 5.7 %collective-permute-start.15 = (f32[8,66,1]{2,1,0:T(8,128)S(1)}, f32[8,66,1]{2,1,0:T(8,128)}, u32[]{:S(2)}, u32[]{:S(2)}) collective-permute-start(f32[8,66,1]{2,1,0:T(8,128)S(1)} %get-tuple-element.20), channel_id=1, source_target_pairs={{0,1},{1,2},{2,3},{4,5},{5,6},{6,7},{8,9},{9,10},{10,11},{12,13},{... | collective-permute-start | bytes 6344 | tf_op jit(solution)/shard_map/ppermute | solution.py:20
  104.6 2.2 collective-permute-done.14
  109.9 4.6 %copy.22 = f32[8,64,256]{0,2,1:T(8,128)} copy(f32[8,64,256]{2,1,0:T(8,128)S(1)} %fusion.5) | data formatting | bytes 1048576 | tf_op jit(solution)/shard_map/sub | solution.py:46
  114.5 4.1 gather_fusion
  118.8 13.1 %all_gather.6 = f32[64,256]{1,0:T(8,128)S(1)} all-gather(f32[8,256]{1,0:T(8,128)S(1)} %copy.23), channel_id=1, replica_groups=mesh['ens'=8,'row'=16,'col'=4] {'ens'}, dimensions={0}, use_global_device_ids=true | all-gather | bytes 73728 | tf_op jit(solution)/shard_map/all_gather | solution.py:65
  132.4 301.1 %all-reduce = (f32[64,64]{1,0:T(8,128)S(1)}, f32[64,64]{1,0:T(8,128)S(1)}) all-reduce(f32[64,64]{1,0:T(8,128)S(1)} %fusion.47, f32[64,64]{1,0:T(8,128)S(1)} %fusion.49), channel_id=1, replica_groups=mesh['ens'=8,'row'=16,'col'=4] {'row','col'}, use_global_device_ids=true, to_apply=%region_4.5 | all-reduce | flops 8192 | bytes 65536 | tf_op jit(solution)/shard_map/psum | solution.py:76
  433.6 5.8 %cholesky.17 = f32[64,64]{1,0:T(8,128)S(1)} custom-call(f32[64,64]{1,0:T(8,128)S(1)} %fusion.58), custom_call_target="Cholesky" | custom-call | tf_op jit(solution)/shard_map/jit(cholesky)/cholesky | solution.py:79
  440.8 4.9 %custom-call.10 = f32[1,64,64]{1,2,0:T(8,128)S(1)} custom-call(f32[1,64,64]{2,1,0:T(8,128)S(1)} %fusion.51), custom_call_target="InvertDiagBlocksLowerTriangular" | custom-call | tf_op jit(solution)/shard_map/jit(_cho_solve)/triangular_solve | solution.py:80
  446.9 4.0 convolution_add_fusion
  (71 shorter events, 32.2 us)
Async XLA Ops:
  7.2 28.2 %copy-start.2 = (f32[64,256]{1,0:T(8,128)S(1)}, f32[64,256]{1,0:T(8,128)}, u32[]{:S(2)}) copy-start(f32[64,256]{1,0:T(8,128)} %param.7) | copy-start | bytes 196612
  7.2 28.2 %copy-start = (f32[2,64,256]{2,1,0:T(8,128)S(1)}, f32[2,64,256]{2,1,0:T(8,128)}, u32[]{:S(2)}) copy-start(f32[2,64,256]{2,1,0:T(8,128)} %param.8) | copy-start | bytes 393220
  7.2 439.7 %all-gather.2.cloned.1.call-start = ((), (), s32[]{:S(2)}) async-start(), calls=%async_computation | async-start | bytes 4718592 | tf_op jit(solution)/shard_map/all_gather | solution.py:86
  11.3 7.1 %collective-permute-start = (f32[11,1,256]{2,1,0:T(1,128)S(1)}, f32[11,1,256]{2,1,0:T(1,128)S(1)}, u32[]{:S(2)}, u32[]{:S(2)}) collective-permute-start(f32[11,1,256]{2,1,0:T(1,128)S(1)} %get-tuple-element.17), channel_id=1, source_target_pairs={{0,4},{4,8},{8,12},{12,16},{16,20},{20,24},{24,28},{28,32},{32,36}... | collective-permute-start | bytes 33800 | tf_op jit(solution)/shard_map/ppermute | solution.py:20
  14.7 5.6 %collective-permute-start.1 = (f32[11,1,256]{2,1,0:T(1,128)S(1)}, f32[11,1,256]{2,1,0:T(1,128)S(1)}, u32[]{:S(2)}, u32[]{:S(2)}) collective-permute-start(f32[11,1,256]{2,1,0:T(1,128)S(1)} %get-tuple-element.18), channel_id=1, source_target_pairs={{4,0},{8,4},{12,8},{16,12},{20,16},{24,20},{28,24},{32,28},{36,32}... | collective-permute-start | bytes 33800 | tf_op jit(solution)/shard_map/ppermute | solution.py:21
  21.5 9.8 %collective-permute-start.2 = (f32[11,66,1]{2,1,0:T(8,128)S(1)}, f32[11,66,1]{2,1,0:T(8,128)S(1)}, u32[]{:S(2)}, u32[]{:S(2)}) collective-permute-start(f32[11,66,1]{2,1,0:T(8,128)S(1)} %get-tuple-element.15), channel_id=1, source_target_pairs={{0,1},{1,2},{2,3},{4,5},{5,6},{6,7},{8,9},{9,10},{10,11},{12,13},{... | collective-permute-start | bytes 8720 | tf_op jit(solution)/shard_map/ppermute | solution.py:20
  24.1 11.3 %collective-permute-start.3 = (f32[11,66,1]{2,1,0:T(8,128)S(1)}, f32[11,66,1]{2,1,0:T(8,128)S(1)}, u32[]{:S(2)}, u32[]{:S(2)}) collective-permute-start(f32[11,66,1]{2,1,0:T(8,128)S(1)} %get-tuple-element.16), channel_id=1, source_target_pairs={{1,0},{2,1},{3,2},{5,4},{6,5},{7,6},{9,8},{10,9},{11,10},{13,12},{... | collective-permute-start | bytes 8720 | tf_op jit(solution)/shard_map/ppermute | solution.py:21
  36.4 38.1 %copy-start.3 = (s32[1,1,256]{2,1,0:T(1,128)S(1)}, s32[1,1,256]{2,1,0:T(1,128)}, u32[]{:S(2)}) copy-start(s32[1,1,256]{2,1,0:T(1,128)} %param.9) | copy-start | bytes 3076
  36.4 6.8 %collective-permute-start.4 = (f32[8,1,256]{2,1,0:T(1,128)S(1)}, f32[8,1,256]{2,1,0:T(1,128)S(1)}, u32[]{:S(2)}, u32[]{:S(2)}) collective-permute-start(f32[8,1,256]{2,1,0:T(1,128)S(1)} %get-tuple-element.29), channel_id=1, source_target_pairs={{4,0},{8,4},{12,8},{16,12},{20,16},{24,20},{28,24},{32,28},{36,32}... | collective-permute-start | bytes 24584 | tf_op jit(solution)/shard_map/ppermute | solution.py:21
  41.3 6.8 %collective-permute-start.5 = (f32[8,1,256]{2,1,0:T(1,128)S(1)}, f32[8,1,256]{2,1,0:T(1,128)S(1)}, u32[]{:S(2)}, u32[]{:S(2)}) collective-permute-start(f32[8,1,256]{2,1,0:T(1,128)S(1)} %get-tuple-element.30), channel_id=1, source_target_pairs={{0,4},{4,8},{8,12},{12,16},{16,20},{20,24},{24,28},{28,32},{32,36}... | collective-permute-start | bytes 24584 | tf_op jit(solution)/shard_map/ppermute | solution.py:20
  48.3 8.6 %collective-permute-start.6 = (f32[8,66,1]{2,1,0:T(8,128)S(1)}, f32[8,66,1]{2,1,0:T(8,128)S(1)}, u32[]{:S(2)}, u32[]{:S(2)}) collective-permute-start(f32[8,66,1]{2,1,0:T(8,128)S(1)} %get-tuple-element.23), channel_id=1, source_target_pairs={{1,0},{2,1},{3,2},{5,4},{6,5},{7,6},{9,8},{10,9},{11,10},{13,12},{... | collective-permute-start | bytes 6344 | tf_op jit(solution)/shard_map/ppermute | solution.py:21
  49.6 8.8 %collective-permute-start.7 = (f32[8,66,1]{2,1,0:T(8,128)S(1)}, f32[8,66,1]{2,1,0:T(8,128)S(1)}, u32[]{:S(2)}, u32[]{:S(2)}) collective-permute-start(f32[8,66,1]{2,1,0:T(8,128)S(1)} %get-tuple-element.24), channel_id=1, source_target_pairs={{0,1},{1,2},{2,3},{4,5},{5,6},{6,7},{8,9},{9,10},{10,11},{12,13},{... | collective-permute-start | bytes 6344 | tf_op jit(solution)/shard_map/ppermute | solution.py:20
  59.2 5.9 %collective-permute-start.8 = (f32[8,1,256]{2,1,0:T(1,128)S(1)}, f32[8,1,256]{2,1,0:T(1,128)S(1)}, u32[]{:S(2)}, u32[]{:S(2)}) collective-permute-start(f32[8,1,256]{2,1,0:T(1,128)S(1)} %get-tuple-element.27), channel_id=1, source_target_pairs={{4,0},{8,4},{12,8},{16,12},{20,16},{24,20},{28,24},{32,28},{36,32}... | collective-permute-start | bytes 24584 | tf_op jit(solution)/shard_map/ppermute | solution.py:21
  61.2 6.8 %collective-permute-start.9 = (f32[8,1,256]{2,1,0:T(1,128)S(1)}, f32[8,1,256]{2,1,0:T(1,128)S(1)}, u32[]{:S(2)}, u32[]{:S(2)}) collective-permute-start(f32[8,1,256]{2,1,0:T(1,128)S(1)} %get-tuple-element.28), channel_id=1, source_target_pairs={{0,4},{4,8},{8,12},{12,16},{16,20},{20,24},{24,28},{28,32},{32,36}... | collective-permute-start | bytes 24584 | tf_op jit(solution)/shard_map/ppermute | solution.py:20
  68.1 9.1 %collective-permute-start.10 = (f32[8,66,1]{2,1,0:T(8,128)S(1)}, f32[8,66,1]{2,1,0:T(8,128)S(1)}, u32[]{:S(2)}, u32[]{:S(2)}) collective-permute-start(f32[8,66,1]{2,1,0:T(8,128)S(1)} %get-tuple-element.21), channel_id=1, source_target_pairs={{1,0},{2,1},{3,2},{5,4},{6,5},{7,6},{9,8},{10,9},{11,10},{13,12},{... | collective-permute-start | bytes 6344 | tf_op jit(solution)/shard_map/ppermute | solution.py:21
  69.4 9.2 %collective-permute-start.11 = (f32[8,66,1]{2,1,0:T(8,128)S(1)}, f32[8,66,1]{2,1,0:T(8,128)S(1)}, u32[]{:S(2)}, u32[]{:S(2)}) collective-permute-start(f32[8,66,1]{2,1,0:T(8,128)S(1)} %get-tuple-element.22), channel_id=1, source_target_pairs={{0,1},{1,2},{2,3},{4,5},{5,6},{6,7},{8,9},{9,10},{10,11},{12,13},{... | collective-permute-start | bytes 6344 | tf_op jit(solution)/shard_map/ppermute | solution.py:20
  79.6 7.5 %collective-permute-start.12 = (f32[8,1,256]{2,1,0:T(1,128)S(1)}, f32[8,1,256]{2,1,0:T(1,128)S(1)}, u32[]{:S(2)}, u32[]{:S(2)}) collective-permute-start(f32[8,1,256]{2,1,0:T(1,128)S(1)} %get-tuple-element.25), channel_id=1, source_target_pairs={{4,0},{8,4},{12,8},{16,12},{20,16},{24,20},{28,24},{32,28},{36,32}... | collective-permute-start | bytes 24584 | tf_op jit(solution)/shard_map/ppermute | solution.py:21
  85.1 11.6 %collective-permute-start.13 = (f32[8,1,256]{2,1,0:T(1,128)S(1)}, f32[8,1,256]{2,1,0:T(1,128)S(1)}, u32[]{:S(2)}, u32[]{:S(2)}) collective-permute-start(f32[8,1,256]{2,1,0:T(1,128)S(1)} %get-tuple-element.26), channel_id=1, source_target_pairs={{0,4},{4,8},{8,12},{12,16},{16,20},{20,24},{24,28},{28,32},{32,36}... | collective-permute-start | bytes 24584 | tf_op jit(solution)/shard_map/ppermute | solution.py:20
  97.6 9.3 %collective-permute-start.14 = (f32[8,66,1]{2,1,0:T(8,128)}, f32[8,66,1]{2,1,0:T(8,128)S(1)}, u32[]{:S(2)}, u32[]{:S(2)}) collective-permute-start(f32[8,66,1]{2,1,0:T(8,128)} %get-tuple-element.19), channel_id=1, source_target_pairs={{1,0},{2,1},{3,2},{5,4},{6,5},{7,6},{9,8},{10,9},{11,10},{13,12},{... | collective-permute-start | bytes 6344 | tf_op jit(solution)/shard_map/ppermute | solution.py:21
  98.9 9.2 %collective-permute-start.15 = (f32[8,66,1]{2,1,0:T(8,128)S(1)}, f32[8,66,1]{2,1,0:T(8,128)}, u32[]{:S(2)}, u32[]{:S(2)}) collective-permute-start(f32[8,66,1]{2,1,0:T(8,128)S(1)} %get-tuple-element.20), channel_id=1, source_target_pairs={{0,1},{1,2},{2,3},{4,5},{5,6},{6,7},{8,9},{9,10},{10,11},{12,13},{... | collective-permute-start | bytes 6344 | tf_op jit(solution)/shard_map/ppermute | solution.py:20
  109.9 22.1 %copy-start.5 = (f32[1,1,256]{2,1,0:T(1,128)S(1)}, f32[1,1,256]{2,1,0:T(1,128)}, u32[]{:S(2)}) copy-start(f32[1,1,256]{2,1,0:T(1,128)} %param.11) | copy-start | bytes 3076
  109.9 22.3 %copy-start.4 = (f32[1,1,256]{2,1,0:T(1,128)S(1)}, f32[1,1,256]{2,1,0:T(1,128)}, u32[]{:S(2)}) copy-start(f32[1,1,256]{2,1,0:T(1,128)} %param.10) | copy-start | bytes 3076
  109.9 337.0 %copy-start.1 = (f32[8,64,256]{2,1,0:T(8,128)S(1)}, f32[8,64,256]{2,1,0:T(8,128)}, u32[]{:S(2)}) copy-start(f32[8,64,256]{2,1,0:T(8,128)} %param.6) | copy-start | bytes 1572868
Sparse Core Ops, SparseCore 0:
  10.7 38.8 all-gather.1
where the time goes:
time: 460 us; the launch traced here: 459 us
  blocking collectives  314 us (68%)
  starting transfers between devices  50.3 us (11%)
  waiting for transfers between devices  41.2 us (9%)
  other arithmetic  18.8 us (4%)
  local copies, waits for them, and re-layouts  15.1 us (3%)
  between operations  14.5 us (3%)
  matrix products  4.8 us (1%)
    psum x1, blocking collectives, shards(): gram, cross = lax.psum((gram_part, cross_part), ('row', 'col'))  301 us
    ppermute x8, starting transfers between devices, padded_2(): before = lax.ppermute(last, axis, up)  29.1 us
    ppermute x8, waiting for transfers between devices, padded_2(): before = lax.ppermute(last, axis, up)  27.4 us
    ppermute x8, starting transfers between devices, padded_2(): after = lax.ppermute(leading, axis, down)  21.2 us
    ppermute x8, waiting for transfers between devices, padded_2(): after = lax.ppermute(leading, axis, down)  13.7 us
    all_gather x1, blocking collectives, shards(): everyone = lax.all_gather(predicted, 'ens', axis=0, tiled=True)  13.1 us
  transfers between devices with their start and end apart: 17, of which 12 were waited for; matrix products, arithmetic and copies ran while one was open for 7% of the time, Pallas kernels for 0%

commit v1 on v0

v1 whole, which is shorter than its diff:
```python
import functools

import jax
import jax.numpy as jnp
from jax import lax
from jax.experimental import pallas as pl
from jax.experimental.pallas import tpu as pltpu
from jax.sharding import PartitionSpec as P

STEPS = 4
diffuse_rate = 0.07
advect_rate = 0.3

MESH = pl.DeviceIdType.MESH
HALO = 4
LANES = 128


def roll(x, shift, axis):
    shift = shift % x.shape[axis]
    return x if shift == 0 else pltpu.roll(x, shift, axis)


def split_bf16(x):
    hi = x.astype(jnp.bfloat16)
    lo = (x - hi.astype(jnp.float32)).astype(jnp.bfloat16)
    return hi, lo


def dot32(a, b):
    return jnp.dot(a, b, preferred_element_type=jnp.float32)


def kernel(
    sizes,
    theta, initial, velocity, sensors, target, noise,
    out, pred,
    blocks, extra, sens_v, targ_v, noise_v,
    row_send, row_recv, col_send, col_recv, corner_recv,
    ext, field, preds, zbuf, ybuf, gall, result,
    load_sem, halo_ssem, halo_rsem, pred_ssem, pred_rsem,
    z_ssem, z_rsem, y_ssem, y_rsem, g_ssem, g_rsem,
    th_ssem, th_rsem, out_sem,
):
    n_e, n_r, n_c, n_z = sizes
    n_x = n_e // 2
    n_yh = n_r // n_z
    n_y = n_yh * n_c
    mem, rows, cols = theta.shape
    rext, cext = rows + 2 * HALO, cols + LANES
    planes = mem + 3
    e, r, c = lax.axis_index("ens"), lax.axis_index("row"), lax.axis_index("col")
    x, core = e // 2, e % 2
    yh, z = r // n_z, r % n_z
    y = yh * n_c + c

    loads = [
        pltpu.make_async_copy(theta, blocks.at[e], load_sem.at[0]),
        pltpu.make_async_copy(initial, extra.at[0], load_sem.at[1]),
        pltpu.make_async_copy(velocity, extra.at[pl.ds(1, 2)], load_sem.at[2]),
        pltpu.make_async_copy(sensors, sens_v, load_sem.at[3]),
        pltpu.make_async_copy(target, targ_v, load_sem.at[4]),
        pltpu.make_async_copy(noise, noise_v, load_sem.at[5]),
    ]
    for copy in loads:
        copy.start()

    prev, nxt = (r + n_r - 1) % n_r, (r + 1) % n_r
    left, right = (c + n_c - 1) % n_c, (c + 1) % n_c
    halo_ids = [
        {"row": prev}, {"row": nxt}, {"col": left}, {"col": right},
        {"row": prev, "col": left}, {"row": prev, "col": right},
        {"row": nxt, "col": left}, {"row": nxt, "col": right},
    ]
    ens_ids = [{"ens": (e + d) % n_e} for d in range(1, n_e)]
    z_ids = [{"row": yh * n_z + (z + d) % n_z} for d in range(1, n_z)]
    y_ids = []
    for d in range(1, n_y):
        other = (y + d) % n_y
        y_ids.append({"row": (other // n_c) * n_z + z, "col": other % n_c})

    barrier = pltpu.get_barrier_semaphore()
    everyone = halo_ids + ens_ids + z_ids + y_ids
    for device in everyone:
        pl.semaphore_signal(barrier, inc=1, device_id=device, device_id_type=MESH)
    pl.semaphore_wait(barrier, len(everyone))

    sends = []

    def remote(src, dst, ssem, rsem, device):
        copy = pltpu.make_async_remote_copy(
            src_ref=src, dst_ref=dst, send_sem=ssem, recv_sem=rsem,
            device_id=device, device_id_type=MESH,
        )
        return copy

    def send(*args):
        copy = remote(*args)
        copy.start()
        sends.append(copy)
        return copy

    for copy in loads:
        copy.wait()

    half = mem // 2
    x_r, x_l, x_f = (x + 1) % n_x, (x + n_x - 1) % n_x, (x + 2) % n_x
    to_r, to_l = {"ens": x_r * 2 + core}, {"ens": x_l * 2 + core}
    to_o = {"ens": x * 2 + (1 - core)}

    def part(index, h):
        return blocks.at[index, pl.ds(h * half, half)]

    def send_half(index, h, slot, device):
        return send(part(index, h), part(index, h), th_ssem.at[slot], th_rsem.at[slot], device)

    sub = lax.broadcasted_iota(jnp.int32, (8, cols), 0)
    low_sub = sub < HALO

    def plane(p):
        return blocks.at[e, p] if p < mem else extra.at[p - mem]

    for pair in range((planes + 1) // 2):
        a, b = 2 * pair, min(2 * pair + 1, planes - 1)
        fa, fb = plane(a)[0:8, :], plane(b)[0:8, :]
        la, lb = plane(a)[rows - 8 : rows, :], plane(b)[rows - 8 : rows, :]
        row_send[0, pair] = jnp.where(low_sub, fa, roll(fb, HALO, 0))
        row_send[1, pair] = jnp.where(low_sub, roll(la, HALO, 0), lb)
    send(row_send.at[0], row_recv.at[0], halo_ssem.at[0], halo_rsem.at[0], halo_ids[0])
    send(row_send.at[1], row_recv.at[1], halo_ssem.at[1], halo_rsem.at[1], halo_ids[1])

    lane = lax.broadcasted_iota(jnp.int32, (rows, LANES), 1)
    slot_of = lane // HALO
    to_left = jnp.zeros((rows, LANES), jnp.float32)
    to_right = jnp.zeros((rows, LANES), jnp.float32)
    for p in range(planes):
        ref = plane(p)
        to_left = jnp.where(slot_of == p, roll(ref[:, 0:LANES], HALO * p, 1), to_left)
        to_right = jnp.where(
            slot_of == p, roll(ref[:, cols - LANES : cols], HALO * p + HALO, 1), to_right
        )
    col_send[0] = to_left
    col_send[1] = to_right
    send(col_send.at[0], col_recv.at[0], halo_ssem.at[2], halo_rsem.at[2], halo_ids[2])
    send(col_send.at[1], col_recv.at[1], halo_ssem.at[3], halo_rsem.at[3], halo_ids[3])
    for k in range(4):
        edge = pl.ds(0, 8) if k < 2 else pl.ds(rows - 8, 8)
        send(
            col_send.at[k % 2, edge], corner_recv.at[k],
            halo_ssem.at[4 + k], halo_rsem.at[4 + k], halo_ids[4 + k],
        )
    halo_copies = list(sends)

    for h in range(2):
        send_half(e, h, h, to_r)
        send_half(e, 1 - h, 2 + 1 - h, to_l)
    for h in range(2):
        send_half(e, h, 4 + h, to_o)

    for p in range(planes):
        ext[p, 0:rows, 0:cols] = plane(p)[...]
    for copy in halo_copies:
        copy.wait_recv()
    for p in range(planes):
        from_next, from_prev = row_recv[0, p // 2], row_recv[1, p // 2]
        if p % 2 == 0:
            tile = jnp.where(low_sub, from_next, roll(from_prev, HALO, 0))
        else:
            tile = jnp.where(low_sub, roll(from_next, HALO, 0), from_prev)
        ext[p, rows:rext, 0:cols] = tile
    low8 = lax.broadcasted_iota(jnp.int32, (8, LANES), 0) < HALO
    from_right = jnp.concatenate(
        [col_recv[0], jnp.where(low8, corner_recv[0], corner_recv[2])], axis=0
    )
    from_left = jnp.concatenate(
        [col_recv[1], jnp.where(low8, corner_recv[1], corner_recv[3])], axis=0
    )
    near = lax.broadcasted_iota(jnp.int32, (rext, LANES), 1) < LANES // 2
    for p in range(planes):
        ext[p, :, cols:cext] = jnp.where(
            near, roll(from_right, -HALO * p, 1), roll(from_left, -HALO - HALO * p, 1)
        )

    ri = lax.broadcasted_iota(jnp.int32, (rext, cext), 0)
    ci = lax.broadcasted_iota(jnp.int32, (rext, cext), 1)
    r_lo = jnp.where(r < n_r - 1, rows + HALO, rows)
    r_hi = jnp.where(r > 0, rows + HALO, rext)
    c_lo = jnp.where(c < n_c - 1, cols + HALO, cols)
    c_hi = jnp.where(c > 0, cext - HALO, cext)
    inside = ((ri < r_lo) | (ri >= r_hi)) & ((ci < c_lo) | (ci >= c_hi))

    ext[mem] = jnp.where(inside, ext[mem], 0.0)
    ext[mem + 1] = jnp.where(inside, (0.5 * advect_rate) * ext[mem + 1], 0.0)
    ext[mem + 2] = jnp.where(inside, (0.5 * advect_rate) * ext[mem + 2], 0.0)

    def forward(m, carry):
        kap = jnp.where(inside, (0.5 * diffuse_rate) * jnp.exp(ext[m]), 0.0)
        v0, v1 = ext[mem + 1], ext[mem + 2]
        f_u, f_d = kap + roll(kap, -1, 0), kap + roll(kap, 1, 0)
        f_r, f_l = kap + roll(kap, -1, 1), kap + roll(kap, 1, 1)
        c_0 = jnp.where(inside, 1.0 - ((f_u + f_d) + (f_r + f_l)), 0.0)
        c_u = jnp.where(inside, f_u - v0, 0.0)
        c_d = jnp.where(inside, f_d + v0, 0.0)
        c_r = jnp.where(inside, f_r - v1, 0.0)
        c_l = jnp.where(inside, f_l + v1, 0.0)
        u = ext[mem]
        for _ in range(STEPS):
            u = (
                c_0 * u
                + (c_u * roll(u, -1, 0) + c_d * roll(u, 1, 0))
                + (c_r * roll(u, -1, 1) + c_l * roll(u, 1, 1))
            )
        field[pl.ds(pl.multiple_of(m * rows, rows), rows), :] = u[0:rows, 0:cols]
        return carry

    lax.fori_loop(0, mem, forward, 0)

    sens = sens_v[0]
    s_col = sens & (cols - 1)
    s_row = sens >> (cols.bit_length() - 1)
    n_s = sens.shape[1]
    hot_c = jnp.where(
        lax.broadcasted_iota(jnp.int32, (cols, n_s), 0) == s_col, 1.0, 0.0
    ).astype(jnp.bfloat16)
    f = field[...]
    f_hi, f_lo = split_bf16(f)
    f_lo2 = ((f - f_hi.astype(jnp.float32)) - f_lo.astype(jnp.float32)).astype(jnp.bfloat16)
    at_cols = dot32(f_hi, hot_c) + (dot32(f_lo, hot_c) + dot32(f_lo2, hot_c))
    hot_r = lax.broadcasted_iota(jnp.int32, (rows, n_s), 0) == s_row
    own = jnp.sum(
        jnp.where(hot_r[None], at_cols.reshape(mem, rows, n_s), 0.0), axis=1
    )
    mine = pl.ds(pl.multiple_of(e * mem, mem), mem)
    preds[mine, :] = own
    for m in range(mem):
        pred[m, 0] = own[m : m + 1]

    def spread(src, dst, ssem, rsem, ids):
        copies = []
        for d, device in enumerate(ids):
            copies.append(send(src, dst, ssem.at[d], rsem.at[d], device))
        return copies

    copies = spread(preds.at[mine], preds.at[mine], pred_ssem, pred_rsem, ens_ids)
    for copy in copies:
        copy.wait_recv()

    flat = preds[...]
    mean = jnp.sum(flat, axis=0, keepdims=True) * (1.0 / (n_e * mem))
    inv_noise = 1.0 / noise_v[0]
    weighted = (flat - mean) * inv_noise
    miss = (targ_v[0] - mean) * inv_noise
    members = n_e * mem
    against = jnp.concatenate(
        [weighted, miss, jnp.zeros((LANES - members - 1, n_s), jnp.float32)], axis=0
    )
    gram = lax.dot_general(
        preds[mine, :] - mean, against, (((1,), (1,)), ((), ())),
        precision=lax.Precision.HIGHEST, preferred_element_type=jnp.float32,
    )

    zbuf[z] = gram
    copies = spread(zbuf.at[z], zbuf.at[z], z_ssem, z_rsem, z_ids)

    def recv_half(slot, index, h):
        remote(part(index, h), part(index, h), th_ssem.at[slot], th_rsem.at[slot], to_o).wait_recv()

    near_l, near_r, far = x_l * 2 + core, x_r * 2 + core, x_f * 2 + core
    recv_half(0, near_l, 0)
    send_half(near_l, 0, 6, to_r)
    recv_half(3, near_r, 1)
    send_half(near_r, 1, 7, to_l)
    recv_half(1, near_l, 1)
    recv_half(2, near_r, 0)
    for h in range(2):
        send_half(near_l, h, 8 + h, to_o)
        send_half(near_r, h, 10 + h, to_o)

    for copy in copies:
        copy.wait_recv()
    ybuf[y] = jnp.sum(zbuf[...], axis=0)
    copies = spread(ybuf.at[y], ybuf.at[y], y_ssem, y_rsem, y_ids)
    for copy in copies:
        copy.wait_recv()
    gall[mine, :] = jnp.sum(ybuf[...], axis=0)
    copies = spread(gall.at[mine], gall.at[mine], g_ssem, g_rsem, ens_ids)

    recv_half(6, far, 0)
    send_half(far, 0, 12, to_o)
    recv_half(7, far, 1)
    send_half(far, 1, 13, to_o)

    for copy in copies:
        copy.wait_recv()

    arow = lax.broadcasted_iota(jnp.int32, (members, LANES), 0)
    acol = lax.broadcasted_iota(jnp.int32, (members, LANES), 1)
    first = members + 8
    unit = (arow == acol) | ((acol >= first) & (acol < first + mem) & (acol - first == arow - e * mem))
    aug = gall[...] * (1.0 / (members - 1)) + jnp.where(unit, 1.0, 0.0)
    for k in range(members):
        row_k = aug[k : k + 1, :]
        scaled = row_k / aug[k : k + 1, k : k + 1]
        col_k = aug[:, k : k + 1]
        aug = jnp.where(arow == k, scaled, aug - col_k * scaled)
    weight = aug[:, first : first + mem] + aug[:, members : members + 1]

    wide = members * 8
    pick = jnp.where(
        lax.broadcasted_iota(jnp.int32, (members, wide), 0)
        == lax.broadcasted_iota(jnp.int32, (members, wide), 1) // 8,
        1.0, 0.0,
    )
    spread_w = lax.dot_general(
        weight, pick, (((0,), (0,)), ((), ())),
        precision=lax.Precision.HIGHEST, preferred_element_type=jnp.float32,
    )
    big = jnp.broadcast_to(spread_w[:, None, :], (mem, 8, wide)).reshape(mem * 8, wide)
    same = (
        lax.broadcasted_iota(jnp.int32, (mem * 8, wide), 0) % 8
        == lax.broadcasted_iota(jnp.int32, (mem * 8, wide), 1) % 8
    )
    big = jnp.where(same, big, 0.0)
    b_hi, b_lo = split_bf16(big)

    recv_half(4, x * 2 + 1 - core, 0)
    recv_half(5, x * 2 + 1 - core, 1)
    for h in range(2):
        recv_half(8 + h, x_l * 2 + 1 - core, h)
        recv_half(10 + h, x_r * 2 + 1 - core, h)
        recv_half(12 + h, x_f * 2 + 1 - core, h)

    outs = []
    for t in range(rows // 8):
        tile = blocks[:, :, 8 * t : 8 * t + 8, :].reshape(wide, cols)
        t_hi, t_lo = split_bf16(tile)
        new = dot32(b_hi, t_hi) + (dot32(b_hi, t_lo) + dot32(b_lo, t_hi))
        result[:, 8 * t : 8 * t + 8, :] = new.reshape(mem, 8, cols)
        copy = pltpu.make_async_copy(
            result.at[:, pl.ds(8 * t, 8)], out.at[:, pl.ds(8 * t, 8)], out_sem.at[t]
        )
        copy.start()
        outs.append(copy)
    for copy in sends:
        copy.wait_send()
    for copy in outs:
        copy.wait()


def shards(sizes, theta, initial, velocity, sensors, target, noise):
    mem, rows, cols = theta.shape
    n_s = sensors.shape[-1]
    n_e, n_r, n_c, n_z = sizes
    n_y = n_r // n_z * n_c
    members = n_e * mem
    planes = mem + 3
    pairs = (planes + 1) // 2
    f32 = jnp.float32
    DMA = pltpu.SemaphoreType.DMA
    return pl.pallas_call(
        functools.partial(kernel, sizes),
        out_shape=(
            jax.ShapeDtypeStruct(theta.shape, f32),
            jax.ShapeDtypeStruct((mem, 1, 1, n_s), f32),
        ),
        in_specs=[pl.BlockSpec(memory_space=pl.ANY)] * 6,
        out_specs=(pl.BlockSpec(memory_space=pl.ANY), pl.BlockSpec(memory_space=pltpu.VMEM)),
        scratch_shapes=[
            pltpu.VMEM((n_e, mem, rows, cols), f32),
            pltpu.VMEM((3, rows, cols), f32),
            pltpu.VMEM((1, 1, n_s), jnp.int32),
            pltpu.VMEM((1, 1, n_s), f32),
            pltpu.VMEM((1, 1, n_s), f32),
            pltpu.VMEM((2, pairs, 8, cols), f32),
            pltpu.VMEM((2, pairs, 8, cols), f32),
            pltpu.VMEM((2, rows, LANES), f32),
            pltpu.VMEM((2, rows, LANES), f32),
            pltpu.VMEM((4, 8, LANES), f32),
            pltpu.VMEM((planes, rows + 2 * HALO, cols + LANES), f32),
            pltpu.VMEM((mem * rows, cols), f32),
            pltpu.VMEM((members, n_s), f32),
            pltpu.VMEM((n_z, mem, LANES), f32),
            pltpu.VMEM((n_y, mem, LANES), f32),
            pltpu.VMEM((members, LANES), f32),
            pltpu.VMEM((mem, rows, cols), f32),
            DMA((6,)),
            DMA((8,)), DMA((8,)),
            DMA((n_e - 1,)), DMA((n_e - 1,)),
            DMA((n_z - 1,)), DMA((n_z - 1,)),
            DMA((n_y - 1,)), DMA((n_y - 1,)),
            DMA((n_e - 1,)), DMA((n_e - 1,)),
            DMA((14,)), DMA((14,)),
            DMA((rows // 8,)),
        ],
        compiler_params=pltpu.CompilerParams(
            collective_id=0, has_side_effects=True, vmem_limit_bytes=48 * 1024 * 1024
        ),
    )(theta, initial, velocity, sensors, target, noise)


def solution(mesh):
    in_specs = (
        P("ens", "row", "col"),
        P("row", "col"),
        P(None, "row", "col"),
        P("row", "col", None),
        P("row", "col", None),
        P("row", "col", None),
    )
    out_specs = (P("ens", "row", "col"), P("ens", "row", "col", None))
    n_r = mesh.shape["row"]
    sizes = (mesh.shape["ens"], n_r, mesh.shape["col"], n_r // 2)
    return jax.shard_map(
        functools.partial(shards, sizes),
        mesh=mesh, in_specs=in_specs, out_specs=out_specs, check_vma=False,
    )
```

time: 460 us -> 61.8 us (0.13)
  the two profiles are of different devices: /device:TPU:288 before, /device:TPU:1 now
where the time goes in v1:
time: 61.8 us; the launch traced here: 61.6 us
  Pallas kernels  54.7 us (89%)
  local copies, waits for them, and re-layouts  6.21 us (10%)
  between operations  0.65 us (1%)
    pallas_call x1, Pallas kernels, shards(): pl.pallas_call(functools.partial(kernel, sizes), out_shape=(jax.ShapeDtyp...  54.7 us
    unnamed x14, local copies, waits for them, and re-layouts  6.21 us

profile of v1, /device:TPU:1, one launch (start us, length us, event | category | flops | bytes accessed | tf_op | source)
XLA Modules:
  0.0 61.6 jit_solution(12919105619749533891)
XLA Ops:
  0.6 0.0 copy-start
  0.6 1.0 %copy-done = f32[8,64,256]{2,1,0:T(8,128)S(1)} copy-done((f32[8,64,256]{2,1,0:T(8,128)S(1)}, f32[8,64,256]{2,1,0:T(8,128)}, u32[]{:S(2)}) %copy-start) | copy-done | bytes 524312
  1.7 0.0 copy-start.1
  1.7 0.9 %copy-done.1 = f32[2,64,256]{2,1,0:T(8,128)S(1)} copy-done((f32[2,64,256]{2,1,0:T(8,128)S(1)}, f32[2,64,256]{2,1,0:T(8,128)}, u32[]{:S(2)}) %copy-start.1) | copy-done | bytes 131096
  2.6 0.0 copy-start.2
  2.6 0.8 %copy-done.2 = f32[64,256]{1,0:T(8,128)S(1)} copy-done((f32[64,256]{1,0:T(8,128)S(1)}, f32[64,256]{1,0:T(8,128)}, u32[]{:S(2)}) %copy-start.2) | copy-done | bytes 65560
  3.4 0.0 copy-start.3
  3.4 0.7 %copy-done.3 = s32[1,1,256]{2,1,0:T(1,128)S(1)} copy-done((s32[1,1,256]{2,1,0:T(1,128)S(1)}, s32[1,1,256]{2,1,0:T(1,128)}, u32[]{:S(2)}) %copy-start.3) | copy-done | bytes 1048
  4.1 0.0 copy-start.4
  4.1 0.7 %copy-done.4 = f32[1,1,256]{2,1,0:T(1,128)S(1)} copy-done((f32[1,1,256]{2,1,0:T(1,128)S(1)}, f32[1,1,256]{2,1,0:T(1,128)}, u32[]{:S(2)}) %copy-start.4) | copy-done | bytes 1048
  4.8 0.0 copy-start.5
  4.8 0.7 %copy-done.5 = f32[1,1,256]{2,1,0:T(1,128)S(1)} copy-done((f32[1,1,256]{2,1,0:T(1,128)S(1)}, f32[1,1,256]{2,1,0:T(1,128)}, u32[]{:S(2)}) %copy-start.5) | copy-done | bytes 1048
  5.5 54.7 %shard_map.77 = (f32[8,64,256]{2,1,0:T(8,128)S(1)}, f32[8,1,1,256]{3,2,1,0:T(1,128)S(1)}) custom-call(f32[8,64,256]{2,1,0:T(8,128)S(1)} %copy-done, f32[64,256]{1,0:T(8,128)S(1)} %copy-done.2, f32[2,64,256]{2,1,0:T(8,128)S(1)} %copy-done.1, s32[1,1,256]{2,1,0:T(1,128)S(1)} %copy-done.3, f32[1,1,256]{2,1,0:T(1,128)S(1)} %copy-done.4, f32[1,1,256]{2,1,0:T(1,128)S(1)} %copy-done.5), custom_call_target="tpu_custom_call" | custom-call | tf_op jit(solution)/shard_map/pallas_call | solution.py:360
  60.2 0.8 %copy.10 = f32[8,64,256]{2,1,0:T(8,128)} copy(f32[8,64,256]{2,1,0:T(8,128)S(1)} %get-tuple-element.4) | data formatting | bytes 1048576
  61.0 0.6 copy.11
Async XLA Ops:
  0.6 1.0 %copy-start = (f32[8,64,256]{2,1,0:T(8,128)S(1)}, f32[8,64,256]{2,1,0:T(8,128)}, u32[]{:S(2)}) copy-start(f32[8,64,256]{2,1,0:T(8,128)} %theta.1) | copy-start | bytes 1572868
  1.7 0.9 %copy-start.1 = (f32[2,64,256]{2,1,0:T(8,128)S(1)}, f32[2,64,256]{2,1,0:T(8,128)}, u32[]{:S(2)}) copy-start(f32[2,64,256]{2,1,0:T(8,128)} %velocity.1) | copy-start | bytes 393220
  2.6 0.8 %copy-start.2 = (f32[64,256]{1,0:T(8,128)S(1)}, f32[64,256]{1,0:T(8,128)}, u32[]{:S(2)}) copy-start(f32[64,256]{1,0:T(8,128)} %initial.1) | copy-start | bytes 196612
  3.4 0.7 %copy-start.3 = (s32[1,1,256]{2,1,0:T(1,128)S(1)}, s32[1,1,256]{2,1,0:T(1,128)}, u32[]{:S(2)}) copy-start(s32[1,1,256]{2,1,0:T(1,128)} %sensors.1) | copy-start | bytes 3076
  4.1 0.7 %copy-start.4 = (f32[1,1,256]{2,1,0:T(1,128)S(1)}, f32[1,1,256]{2,1,0:T(1,128)}, u32[]{:S(2)}) copy-start(f32[1,1,256]{2,1,0:T(1,128)} %target.1) | copy-start | bytes 3076
  4.8 0.7 %copy-start.5 = (f32[1,1,256]{2,1,0:T(1,128)S(1)}, f32[1,1,256]{2,1,0:T(1,128)}, u32[]{:S(2)}) copy-start(f32[1,1,256]{2,1,0:T(1,128)} %noise.1) | copy-start | bytes 3076

commit v2 on v1

v2 whole, which is shorter than its diff:
```python
import functools

import jax
import jax.numpy as jnp
from jax import lax
from jax.experimental import pallas as pl
from jax.experimental.pallas import tpu as pltpu
from jax.sharding import PartitionSpec as P

STEPS = 4
diffuse_rate = 0.07
advect_rate = 0.3

MESH = pl.DeviceIdType.MESH
HALO = 4
LANES = 128


def roll(x, shift, axis):
    shift = shift % x.shape[axis]
    return x if shift == 0 else pltpu.roll(x, shift, axis)


def split_bf16(x):
    hi = x.astype(jnp.bfloat16)
    lo = (x - hi.astype(jnp.float32)).astype(jnp.bfloat16)
    return hi, lo


def dot32(a, b):
    return jnp.dot(a, b, preferred_element_type=jnp.float32)


def eliminate(aug, n, p):
    arow = lax.broadcasted_iota(jnp.int32, aug.shape, 0)
    for k in range(0, n, p):
        col = [jnp.broadcast_to(aug[:, k + j : k + j + 1], aug.shape) for j in range(p)]
        d = [[col[j][k + i : k + i + 1, :] for j in range(p)] for i in range(p)]
        new = [aug[k + i : k + i + 1, :] for i in range(p)]
        for i in range(p):
            inv = 1.0 / d[i][i]
            for j in range(i + 1, p):
                d[i][j] = d[i][j] * inv
            new[i] = new[i] * inv
            for q in range(p):
                if q != i:
                    for j in range(i + 1, p):
                        d[q][j] = d[q][j] - d[q][i] * d[i][j]
                    new[q] = new[q] - d[q][i] * new[i]
        less = col[0] * new[0]
        for j in range(1, p):
            less = less + col[j] * new[j]
        aug = aug - less
        for j in range(p):
            aug = jnp.where(arow == k + j, new[j], aug)
    return aug


def kernel(
    sizes,
    theta, initial, velocity, sensors, target, noise,
    out, pred,
    blocks, logk, extra, frame, sens_v, targ_v, noise_v,
    col_send, col_recv, corner_recv,
    kap, c_0, c_u, c_d, c_r, c_l, u_0, u_1, u_2, u_3, field,
    preds, zbuf, ybuf, gall, result,
    load_sem, halo_ssem, halo_rsem, pred_ssem, pred_rsem,
    z_ssem, z_rsem, y_ssem, y_rsem, g_ssem, g_rsem,
    th_ssem, th_rsem, out_sem,
):
    n_e, n_r, n_c, n_z = sizes
    n_x = n_e // 2
    n_yh = n_r // n_z
    n_y = n_yh * n_c
    mem, rows, cols = theta.shape
    cext = cols + LANES
    e, r, c = lax.axis_index("ens"), lax.axis_index("row"), lax.axis_index("col")
    x, core = e // 2, e % 2
    yh, z = r // n_z, r % n_z
    y = yh * n_c + c

    loads = [
        pltpu.make_async_copy(theta, blocks.at[e], load_sem.at[0]),
        pltpu.make_async_copy(initial, extra.at[0, pl.ds(8, rows)], load_sem.at[1]),
        pltpu.make_async_copy(
            velocity, extra.at[pl.ds(1, 2), pl.ds(8, rows)], load_sem.at[2]
        ),
        pltpu.make_async_copy(sensors, sens_v, load_sem.at[3]),
        pltpu.make_async_copy(target, targ_v, load_sem.at[4]),
        pltpu.make_async_copy(noise, noise_v, load_sem.at[5]),
    ]
    for copy in loads:
        copy.start()

    prev, nxt = (r + n_r - 1) % n_r, (r + 1) % n_r
    left, right = (c + n_c - 1) % n_c, (c + 1) % n_c
    halo_ids = [
        {"row": prev}, {"row": nxt}, {"col": left}, {"col": right},
        {"row": prev, "col": left}, {"row": prev, "col": right},
        {"row": nxt, "col": left}, {"row": nxt, "col": right},
    ]
    ens_ids = [{"ens": (e + d) % n_e} for d in range(1, n_e)]
    z_ids = [{"row": yh * n_z + (z + d) % n_z} for d in range(1, n_z)]
    y_ids = []
    for dy in sorted(range(n_y), key=lambda d: -min(d, n_y - d)):
        for dx in sorted(range(n_x), key=lambda d: -min(d, n_x - d)):
            if dx or dy:
                other = (y + dy) % n_y
                y_ids.append({
                    "ens": (x + dx) % n_x * 2 + core,
                    "row": other // n_c * n_z + z,
                    "col": other % n_c,
                })

    barrier = pltpu.get_barrier_semaphore()
    everyone = halo_ids + ens_ids + z_ids + y_ids
    for device in everyone:
        pl.semaphore_signal(barrier, inc=1, device_id=device, device_id_type=MESH)
    pl.semaphore_wait(barrier, len(everyone))

    sends = []

    def remote(src, dst, ssem, rsem, device):
        copy = pltpu.make_async_remote_copy(
            src_ref=src, dst_ref=dst, send_sem=ssem, recv_sem=rsem,
            device_id=device, device_id_type=MESH,
        )
        return copy

    def send(*args):
        copy = remote(*args)
        copy.start()
        sends.append(copy)
        return copy

    for copy in loads:
        copy.wait()

    half = mem // 2
    x_r, x_l, x_f = (x + 1) % n_x, (x + n_x - 1) % n_x, (x + 2) % n_x
    to_r, to_l = {"ens": x_r * 2 + core}, {"ens": x_l * 2 + core}
    to_o = {"ens": x * 2 + (1 - core)}

    def part(index, h):
        return blocks.at[index, pl.ds(h * half, half)]

    def send_half(index, h, slot, device):
        return send(part(index, h), part(index, h), th_ssem.at[slot], th_rsem.at[slot], device)

    def turned(t):
        tile = blocks[e, :, 8 * t : 8 * t + 8, :]
        logk[HALO + 8 * t : HALO + 8 * t + 8] = jnp.swapaxes(tile, 0, 1)

    last = rows // 8 - 1
    turned(0)
    turned(last)

    def send_halo(k, src, dst, device):
        send(src, dst, halo_ssem.at[k], halo_rsem.at[k], device)

    def edge(start):
        return logk.at[pl.ds(start, HALO)]

    def edge_x(start):
        return extra.at[:, pl.ds(start, 8)]

    send_halo(0, edge(HALO), edge(rows + HALO), halo_ids[0])
    send_halo(1, edge(rows), edge(0), halo_ids[1])
    send_halo(2, edge_x(8), edge_x(rows + 8), halo_ids[0])
    send_halo(3, edge_x(rows), edge_x(0), halo_ids[1])
    for t in range(1, last):
        turned(t)

    lane = lax.broadcasted_iota(jnp.int32, (8, LANES), 1)
    slot_of = lane // HALO
    per = LANES // HALO
    for side in range(2):
        low = 0 if side == 0 else cols - LANES
        off = 0 if side == 0 else HALO
        for half_t, first_row in ((0, 0), (2, per)):
            acc = jnp.zeros((8, LANES), jnp.float32)
            for k in range(per):
                row = logk[HALO + first_row + k, :, low : low + LANES]
                acc = jnp.where(slot_of == k, roll(row, HALO * k + off, 1), acc)
            col_send[side, half_t] = acc
        acc = jnp.zeros((8, LANES), jnp.float32)
        for p in range(3):
            for t in range(last + 1):
                k = p * (last + 1) + t
                row = extra[p, 8 + 8 * t : 16 + 8 * t, low : low + LANES]
                acc = jnp.where(slot_of == k, roll(row, HALO * k + off, 1), acc)
        col_send[side, 1] = acc
        send_halo(4 + side, col_send.at[side], col_recv.at[side], halo_ids[2 + side])
    for k in range(4):
        part_k = pl.ds(0 if k < 2 else 1, 2)
        send_halo(6 + k, col_send.at[k % 2, part_k], corner_recv.at[k], halo_ids[4 + k])
    halo_copies = list(sends)

    for h in range(2):
        send_half(e, h, h, to_r)
        send_half(e, 1 - h, 2 + 1 - h, to_l)
    for h in range(2):
        send_half(e, h, 4 + h, to_o)

    ci = lax.broadcasted_iota(jnp.int32, (8, cext), 1)
    c_lo = jnp.where(c < n_c - 1, cols + HALO, cols)
    c_hi = jnp.where(c > 0, cext - HALO, cext)
    ok_mid = (ci < c_lo) | (ci >= c_hi)
    ok_top = ok_mid & (r > 0)
    ok_bot = ok_mid & (r < n_r - 1)
    near = lane < LANES // 2
    half_d, half_a = 0.5 * diffuse_rate, 0.5 * advect_rate

    def unpack(from_right, from_left, k):
        return jnp.where(near, roll(from_right, -HALO * k, 1), roll(from_left, -HALO - HALO * k, 1))

    def fill_kap(i, ok, from_right, from_left, k):
        kap[i, :, 0:cols] = jnp.where(ok[:, 0:cols], half_d * jnp.exp(logk[i]), 0.0)
        outer = unpack(from_right, from_left, k)
        kap[i, :, cols:cext] = jnp.where(ok[:, cols:cext], half_d * jnp.exp(outer), 0.0)

    def fill_extra(t, ok, from_right, from_left, slot_t):
        at = slice(8 * t, 8 * t + 8)
        for p in range(3):
            scale = 1.0 if p == 0 else half_a
            outer = unpack(from_right, from_left, p * (last + 1) + slot_t)
            frame[p, at, 0:cols] = jnp.where(ok[:, 0:cols], scale * extra[p, at], 0.0)
            frame[p, at, cols:cext] = jnp.where(ok[:, cols:cext], scale * outer, 0.0)

    def coefficients(i, ok, v0, v1):
        k = kap[i]
        f_u, f_d = k + kap[i + 1], k + kap[i - 1]
        f_r, f_l = k + roll(k, -1, 1), k + roll(k, 1, 1)
        c_0[i] = jnp.where(ok, 1.0 - ((f_u + f_d) + (f_r + f_l)), 0.0)
        c_u[i] = jnp.where(ok, f_u - v0, 0.0)
        c_d[i] = jnp.where(ok, f_d + v0, 0.0)
        c_r[i] = jnp.where(ok, f_r - v1, 0.0)
        c_l[i] = jnp.where(ok, f_l + v1, 0.0)

    def step(src, i):
        u = src[i]
        return (
            c_0[i] * u
            + (c_u[i] * src[i + 1] + c_d[i] * src[i - 1])
            + (c_r[i] * roll(u, -1, 1) + c_l[i] * roll(u, 1, 1))
        )

    states = [u_0, u_1, u_2, u_3]

    for copy in halo_copies[4:6]:
        copy.wait_recv()
    for t in range(last + 1):
        fill_extra(t + 1, ok_mid, col_recv[0, 1], col_recv[1, 1], t)
    for i in range(rows):
        tile = 0 if i < per else 2
        fill_kap(HALO + i, ok_mid, col_recv[0, tile], col_recv[1, tile], i % per)

    def first(t, carry):
        at = pl.ds(pl.multiple_of(8 * t + 8, 8), 8)
        u, v0, v1 = frame[0, at, :], frame[1, at, :], frame[2, at, :]
        for j in range(8):
            i = HALO + 8 * t + j
            u_0[i] = jnp.broadcast_to(u[j : j + 1], (8, cext))
            coefficients(i, ok_mid, v0[j : j + 1], v1[j : j + 1])
        return carry

    lax.fori_loop(0, last + 1, first, 0)
    for s in range(STEPS):
        def chunk(t, carry, s=s):
            for j in range(8):
                i = HALO + 8 * t + j
                new = step(states[s], i)
                if s < STEPS - 1:
                    states[s + 1][i] = new
                else:
                    field[pl.ds(pl.multiple_of(64 * t + 8 * j, 8), 8), :] = new[:, 0:cols]
            return carry
        lax.fori_loop(0, last + 1, chunk, 0)

    sens = sens_v[0]
    n_s = sens.shape[1]
    s_col = sens & (cols - 1)
    s_row = jnp.broadcast_to(sens >> (cols.bit_length() - 1), (8, n_s))
    hot_c = jnp.where(
        lax.broadcasted_iota(jnp.int32, (cols, n_s), 0) == s_col, 1.0, 0.0
    ).astype(jnp.bfloat16)

    def sensed(first_row, count, acc):
        f = field[8 * first_row : 8 * (first_row + count), :]
        f_hi, f_lo = split_bf16(f)
        f_lo2 = ((f - f_hi.astype(jnp.float32)) - f_lo.astype(jnp.float32)).astype(jnp.bfloat16)
        at = dot32(f_hi, hot_c) + (dot32(f_lo, hot_c) + dot32(f_lo2, hot_c))
        for j in range(count):
            acc = jnp.where(s_row == first_row + j, at[8 * j : 8 * j + 8], acc)
        return acc

    own = sensed(8, rows - 16, jnp.zeros((mem, n_s), jnp.float32))

    for copy in halo_copies[0:4] + halo_copies[6:10]:
        copy.wait_recv()
    fill_extra(0, ok_top, corner_recv[2, 0], corner_recv[3, 0], last)
    fill_extra(last + 2, ok_bot, corner_recv[0, 1], corner_recv[1, 1], 0)
    for k in range(HALO):
        fill_kap(k, ok_top, corner_recv[2, 1], corner_recv[3, 1], per - HALO + k)
        fill_kap(HALO + rows + k, ok_bot, corner_recv[0, 0], corner_recv[1, 0], k)

    def row_of(p, i):
        return frame[p, i + 4 : i + 5, :]

    for k in range(HALO):
        u_0[k] = jnp.broadcast_to(row_of(0, k), (8, cext))
        i = HALO + rows + k
        u_0[i] = jnp.broadcast_to(row_of(0, i), (8, cext))
    for i in range(1, HALO + 1):
        j = 2 * HALO + rows - 1 - i
        coefficients(i, ok_top if i < HALO else ok_mid, row_of(1, i), row_of(2, i))
        coefficients(j, ok_bot if i < HALO else ok_mid, row_of(1, j), row_of(2, j))
    for s in range(STEPS):
        for i in range(1 + s, HALO + 1 + s):
            j = 2 * HALO + rows - 1 - i
            for q in (i, j):
                new = step(states[s], q)
                if s < STEPS - 1:
                    states[s + 1][q] = new
                else:
                    field[8 * (q - HALO) : 8 * (q - HALO) + 8, :] = new[:, 0:cols]
    own = sensed(0, 8, own)
    own = sensed(rows - 8, 8, own)
    mine = pl.ds(pl.multiple_of(e * mem, mem), mem)
    preds[mine, :] = own
    for m in range(mem):
        pred[m, 0] = own[m : m + 1]

    def spread(src, dst, ssem, rsem, ids):
        copies = []
        for d, device in enumerate(ids):
            copies.append(send(src, dst, ssem.at[d], rsem.at[d], device))
        return copies

    copies = spread(preds.at[mine], preds.at[mine], pred_ssem, pred_rsem, ens_ids)
    for copy in copies:
        copy.wait_recv()

    flat = preds[...]
    mean = jnp.sum(flat, axis=0, keepdims=True) * (1.0 / (n_e * mem))
    inv_noise = 1.0 / noise_v[0]
    weighted = (flat - mean) * inv_noise
    miss = (targ_v[0] - mean) * inv_noise
    members = n_e * mem
    against = jnp.concatenate(
        [weighted, miss, jnp.zeros((LANES - members - 1, n_s), jnp.float32)], axis=0
    )
    gram = lax.dot_general(
        preds[mine, :] - mean, against, (((1,), (1,)), ((), ())),
        precision=lax.Precision.HIGHEST, preferred_element_type=jnp.float32,
    )

    zbuf[z] = gram
    copies = spread(zbuf.at[z], zbuf.at[z], z_ssem, z_rsem, z_ids)

    def recv_half(slot, index, h):
        remote(part(index, h), part(index, h), th_ssem.at[slot], th_rsem.at[slot], to_o).wait_recv()

    near_l, near_r, far = x_l * 2 + core, x_r * 2 + core, x_f * 2 + core
    recv_half(0, near_l, 0)
    send_half(near_l, 0, 6, to_r)
    recv_half(3, near_r, 1)
    send_half(near_r, 1, 7, to_l)
    recv_half(1, near_l, 1)
    recv_half(2, near_r, 0)
    for h in range(2):
        send_half(near_l, h, 8 + h, to_o)
        send_half(near_r, h, 10 + h, to_o)

    for copy in copies:
        copy.wait_recv()
    ybuf[x, y] = jnp.sum(zbuf[...], axis=0)
    copies = spread(ybuf.at[x, y], ybuf.at[x, y], y_ssem, y_rsem, y_ids)
    for copy in copies:
        copy.wait_recv()
    gall[core] = jnp.sum(ybuf[...], axis=1)
    copies = [send(gall.at[core], gall.at[core], g_ssem.at[0], g_rsem.at[0], to_o)]

    recv_half(6, far, 0)
    send_half(far, 0, 12, to_o)
    recv_half(7, far, 1)
    send_half(far, 1, 13, to_o)

    for copy in copies:
        copy.wait_recv()

    arow = lax.broadcasted_iota(jnp.int32, (members, LANES), 0)
    acol = lax.broadcasted_iota(jnp.int32, (members, LANES), 1)
    first = members + 8
    unit = (arow == acol) | ((acol >= first) & (acol < first + mem) & (acol - first == arow - e * mem))
    sums = jnp.concatenate([gall[i % 2, i // 2] for i in range(n_e)], axis=0)
    aug = sums * (1.0 / (members - 1)) + jnp.where(unit, 1.0, 0.0)
    aug = eliminate(aug, members, 8)
    weight = aug[:, first : first + mem] + aug[:, members : members + 1]

    wide = members * 8
    pick = jnp.where(
        lax.broadcasted_iota(jnp.int32, (members, wide), 0)
        == lax.broadcasted_iota(jnp.int32, (members, wide), 1) // 8,
        1.0, 0.0,
    )
    spread_w = lax.dot_general(
        weight, pick, (((0,), (0,)), ((), ())),
        precision=lax.Precision.HIGHEST, preferred_element_type=jnp.float32,
    )
    big = jnp.broadcast_to(spread_w[:, None, :], (mem, 8, wide)).reshape(mem * 8, wide)
    same = (
        lax.broadcasted_iota(jnp.int32, (mem * 8, wide), 0) % 8
        == lax.broadcasted_iota(jnp.int32, (mem * 8, wide), 1) % 8
    )
    big = jnp.where(same, big, 0.0)
    b_hi, b_lo = split_bf16(big)
    b_both = jnp.concatenate([b_hi, b_lo], axis=0)

    recv_half(4, x * 2 + 1 - core, 0)
    recv_half(5, x * 2 + 1 - core, 1)
    for h in range(2):
        recv_half(8 + h, x_l * 2 + 1 - core, h)
        recv_half(10 + h, x_r * 2 + 1 - core, h)
        recv_half(12 + h, x_f * 2 + 1 - core, h)

    outs = []
    for t in range(rows // 8):
        tile = blocks[:, :, 8 * t : 8 * t + 8, :].reshape(wide, cols)
        t_hi, t_lo = split_bf16(tile)
        two = dot32(b_both, t_hi)
        new = two[: mem * 8] + (dot32(b_hi, t_lo) + two[mem * 8 :])
        result[:, 8 * t : 8 * t + 8, :] = new.reshape(mem, 8, cols)
        copy = pltpu.make_async_copy(
            result.at[:, pl.ds(8 * t, 8)], out.at[:, pl.ds(8 * t, 8)], out_sem.at[t]
        )
        copy.start()
        outs.append(copy)
    for copy in sends:
        copy.wait_send()
    for copy in outs:
        copy.wait()


def shards(sizes, theta, initial, velocity, sensors, target, noise):
    mem, rows, cols = theta.shape
    n_s = sensors.shape[-1]
    n_e, n_r, n_c, n_z = sizes
    n_y = n_r // n_z * n_c
    members = n_e * mem
    rext, cext = rows + 2 * HALO, cols + LANES
    f32 = jnp.float32
    DMA = pltpu.SemaphoreType.DMA
    return pl.pallas_call(
        functools.partial(kernel, sizes),
        out_shape=(
            jax.ShapeDtypeStruct(theta.shape, f32),
            jax.ShapeDtypeStruct((mem, 1, 1, n_s), f32),
        ),
        in_specs=[pl.BlockSpec(memory_space=pltpu.HBM)] * 6,
        out_specs=(pl.BlockSpec(memory_space=pltpu.HBM), pl.BlockSpec(memory_space=pltpu.VMEM)),
        scratch_shapes=[
            pltpu.VMEM((n_e, mem, rows, cols), f32),
            pltpu.VMEM((rext, mem, cols), f32),
            pltpu.VMEM((3, rows + 16, cols), f32),
            pltpu.VMEM((3, rows + 16, cext), f32),
            pltpu.VMEM((1, 1, n_s), jnp.int32),
            pltpu.VMEM((1, 1, n_s), f32),
            pltpu.VMEM((1, 1, n_s), f32),
            pltpu.VMEM((2, 3, 8, LANES), f32),
            pltpu.VMEM((2, 3, 8, LANES), f32),
            pltpu.VMEM((4, 2, 8, LANES), f32),
            *[pltpu.VMEM((rext, mem, cext), f32)] * 10,
            pltpu.VMEM((mem * rows, cols), f32),
            pltpu.VMEM((members, n_s), f32),
            pltpu.VMEM((n_z, mem, LANES), f32),
            pltpu.VMEM((n_e // 2, n_y, mem, LANES), f32),
            pltpu.VMEM((2, n_e // 2, mem, LANES), f32),
            pltpu.VMEM((mem, rows, cols), f32),
            DMA((6,)),
            DMA((10,)), DMA((10,)),
            DMA((n_e - 1,)), DMA((n_e - 1,)),
            DMA((n_z - 1,)), DMA((n_z - 1,)),
            DMA((n_e // 2 * n_y - 1,)), DMA((n_e // 2 * n_y - 1,)),
            DMA((1,)), DMA((1,)),
            DMA((14,)), DMA((14,)),
            DMA((rows // 8,)),
        ],
        compiler_params=pltpu.CompilerParams(
            collective_id=0, has_side_effects=True, vmem_limit_bytes=48 * 1024 * 1024
        ),
    )(*(pltpu.with_memory_space_constraint(a, pltpu.HBM)
        for a in (theta, initial, velocity, sensors, target, noise)))


def solution(mesh):
    in_specs = (
        P("ens", "row", "col"),
        P("row", "col"),
        P(None, "row", "col"),
        P("row", "col", None),
        P("row", "col", None),
        P("row", "col", None),
    )
    out_specs = (P("ens", "row", "col"), P("ens", "row", "col", None))
    n_r = mesh.shape["row"]
    sizes = (mesh.shape["ens"], n_r, mesh.shape["col"], n_r // 2)
    return jax.shard_map(
        functools.partial(shards, sizes),
        mesh=mesh, in_specs=in_specs, out_specs=out_specs, check_vma=False,
    )
```

time: 61.8 us -> 51.6 us (0.83)
  Pallas kernels: 54.7 us -> 49.4 us
  local copies, waits for them, and re-layouts: 6.21 us -> 1.39 us
    pallas_call x1, Pallas kernels: 54.7 us -> 49.4 us  [shards(): pl.pallas_call(functools.partial(kernel, sizes), out_shape=(jax.ShapeDtyp...]
    unnamed x14 -> x2, local copies, waits for them, and re-layouts: 6.21 us -> 1.39 us
where the time goes in v2:
time: 51.6 us; the launch traced here: 51.5 us
  Pallas kernels  49.4 us (96%)
  local copies, waits for them, and re-layouts  1.39 us (3%)
  between operations  0.64 us (1%)
    pallas_call x1, Pallas kernels, shards(): pl.pallas_call(functools.partial(kernel, sizes), out_shape=(jax.ShapeDtyp...  49.4 us
    unnamed x2, local copies, waits for them, and re-layouts  1.39 us

profile of v2, /device:TPU:1, one launch (start us, length us, event | category | flops | bytes accessed | tf_op | source)
XLA Modules:
  0.0 51.5 jit_solution(13897321355552545961)
XLA Ops:
  0.6 49.4 %shard_map.77 = (f32[8,64,256]{2,1,0:T(8,128)S(1)}, f32[8,1,1,256]{3,2,1,0:T(1,128)S(1)}) custom-call(f32[8,64,256]{2,1,0:T(8,128)} %theta.1, f32[64,256]{1,0:T(8,128)} %initial.1, f32[2,64,256]{2,1,0:T(8,128)} %velocity.1, s32[1,1,256]{2,1,0:T(1,128)} %sensors.1, f32[1,1,256]{2,1,0:T(1,128)} %target.1, f32[1,1,256]{2,1,0:T(1,128)} %noise.1), custom_call_target="tpu_custom_call" | custom-call | tf_op jit(solution)/shard_map/pallas_call | solution.py:454
  50.1 0.8 %copy.10 = f32[8,64,256]{2,1,0:T(8,128)} copy(f32[8,64,256]{2,1,0:T(8,128)S(1)} %get-tuple-element.4) | data formatting | bytes 1048576
  50.9 0.6 %copy.11 = f32[8,1,1,256]{3,2,1,0:T(1,128)} copy(f32[8,1,1,256]{3,2,1,0:T(1,128)S(1)} %get-tuple-element.5) | data formatting | bytes 16384

commit v3 on v2

--- a/solution.py
+++ b/solution.py
@@ -63,10 +63,10 @@
     blocks, logk, extra, frame, sens_v, targ_v, noise_v,
     col_send, col_recv, corner_recv,
     kap, c_0, c_u, c_d, c_r, c_l, u_0, u_1, u_2, u_3, field,
-    preds, zbuf, ybuf, gall, result,
+    preds, zbuf, ybuf, gall, th_hi, th_lo, result,
     load_sem, halo_ssem, halo_rsem, pred_ssem, pred_rsem,
     z_ssem, z_rsem, y_ssem, y_rsem, g_ssem, g_rsem,
-    th_ssem, th_rsem, out_sem,
+    th_ssem, th_rsem, out_sem, relay_sem,
 ):
     n_e, n_r, n_c, n_z = sizes
     n_x = n_e // 2
@@ -112,12 +112,47 @@
                     "col": other % n_c,
                 })
 
+    has_p, has_n, has_l, has_r = r > 0, r < n_r - 1, c > 0, c < n_c - 1
+    halo_out = [
+        has_p, has_n, has_l, has_r, has_p & has_l, has_p & has_r, has_n & has_l, has_n & has_r
+    ]
+    halo_in = [
+        has_n, has_p, has_r, has_l, has_n & has_r, has_n & has_l, has_p & has_r, has_p & has_l
+    ]
+    x_r, x_l, x_f = (x + 1) % n_x, (x + n_x - 1) % n_x, (x + 2) % n_x
+    to_r, to_l = {"ens": x_r * 2 + core}, {"ens": x_l * 2 + core}
+    to_o = {"ens": x * 2 + (1 - core)}
+    y_r, y_l = (y + 1) % n_y, (y + n_y - 1) % n_y
+    near_ids = [
+        to_r, to_l, to_o,
+        {"row": yh * n_z + (z + 1) % n_z}, {"row": yh * n_z + (z + n_z - 1) % n_z},
+        {"row": y_r // n_c * n_z + z, "col": y_r % n_c},
+        {"row": y_l // n_c * n_z + z, "col": y_l % n_c},
+    ]
+
     barrier = pltpu.get_barrier_semaphore()
-    everyone = halo_ids + ens_ids + z_ids + y_ids
-    for device in everyone:
+    for device in near_ids:
         pl.semaphore_signal(barrier, inc=1, device_id=device, device_id_type=MESH)
-    pl.semaphore_wait(barrier, len(everyone))
-
+    for device, there in zip(halo_ids, halo_out, strict=True):
+        @pl.when(there)
+        def _(device=device):
+            pl.semaphore_signal(barrier, inc=1, device_id=device, device_id_type=MESH)
+    one = [jnp.where(v, 1, 0) for v in (has_p, has_n, has_l, has_r)]
+    n_halo = (1 + one[0] + one[1]) * (1 + one[2] + one[3]) - 1
+    pl.semaphore_wait(barrier, len(near_ids) + n_halo)
+
+    def relay_signal(j):
+        for device in near_ids:
+            pl.semaphore_signal(
+                relay_sem.at[j], inc=1, device_id=device, device_id_type=MESH
+            )
+
+    def relay_wait(j):
+        pl.semaphore_wait(relay_sem.at[j], len(near_ids))
+        if j < 2:
+            relay_signal(j + 1)
+
+    relay_signal(0)
     sends = []
 
     def remote(src, dst, ssem, rsem, device):
@@ -137,9 +172,6 @@
         copy.wait()
 
     half = mem // 2
-    x_r, x_l, x_f = (x + 1) % n_x, (x + n_x - 1) % n_x, (x + 2) % n_x
-    to_r, to_l = {"ens": x_r * 2 + core}, {"ens": x_l * 2 + core}
-    to_o = {"ens": x * 2 + (1 - core)}
 
     def part(index, h):
         return blocks.at[index, pl.ds(h * half, half)]
@@ -155,8 +187,16 @@
     turned(0)
     turned(last)
 
-    def send_halo(k, src, dst, device):
-        send(src, dst, halo_ssem.at[k], halo_rsem.at[k], device)
+    halo_copies = []
+
+    def send_halo(k, src, dst, which):
+        copy = remote(src, dst, halo_ssem.at[k], halo_rsem.at[k], halo_ids[which])
+        pl.when(halo_out[which])(copy.start)
+        halo_copies.append((copy, halo_out[which], halo_in[which]))
+
+    def wait_halo(k):
+        copy, _, there = halo_copies[k]
+        pl.when(there)(copy.wait_recv)
 
     def edge(start):
         return logk.at[pl.ds(start, HALO)]
@@ -164,10 +204,10 @@
     def edge_x(start):
         return extra.at[:, pl.ds(start, 8)]
 
-    send_halo(0, edge(HALO), edge(rows + HALO), halo_ids[0])
-    send_halo(1, edge(rows), edge(0), halo_ids[1])
-    send_halo(2, edge_x(8), edge_x(rows + 8), halo_ids[0])
-    send_halo(3, edge_x(rows), edge_x(0), halo_ids[1])
+    send_halo(0, edge(HALO), edge(rows + HALO), 0)
+    send_halo(1, edge(rows), edge(0), 1)
+    send_halo(2, edge_x(8), edge_x(rows + 8), 0)
+    send_halo(3, edge_x(rows), edge_x(0), 1)
     for t in range(1, last):
         turned(t)
 
@@ -190,11 +230,10 @@
                 row = extra[p, 8 + 8 * t : 16 + 8 * t, low : low + LANES]
                 acc = jnp.where(slot_of == k, roll(row, HALO * k + off, 1), acc)
         col_send[side, 1] = acc
-        send_halo(4 + side, col_send.at[side], col_recv.at[side], halo_ids[2 + side])
+        send_halo(4 + side, col_send.at[side], col_recv.at[side], 2 + side)
     for k in range(4):
         part_k = pl.ds(0 if k < 2 else 1, 2)
-        send_halo(6 + k, col_send.at[k % 2, part_k], corner_recv.at[k], halo_ids[4 + k])
-    halo_copies = list(sends)
+        send_halo(6 + k, col_send.at[k % 2, part_k], corner_recv.at[k], 4 + k)
 
     for h in range(2):
         send_half(e, h, h, to_r)
@@ -247,35 +286,33 @@
 
     states = [u_0, u_1, u_2, u_3]
 
-    for copy in halo_copies[4:6]:
-        copy.wait_recv()
+    relay_wait(0)
+    wait_halo(4)
+    wait_halo(5)
     for t in range(last + 1):
         fill_extra(t + 1, ok_mid, col_recv[0, 1], col_recv[1, 1], t)
     for i in range(rows):
         tile = 0 if i < per else 2
         fill_kap(HALO + i, ok_mid, col_recv[0, tile], col_recv[1, tile], i % per)
 
-    def first(t, carry):
-        at = pl.ds(pl.multiple_of(8 * t + 8, 8), 8)
-        u, v0, v1 = frame[0, at, :], frame[1, at, :], frame[2, at, :]
-        for j in range(8):
-            i = HALO + 8 * t + j
-            u_0[i] = jnp.broadcast_to(u[j : j + 1], (8, cext))
-            coefficients(i, ok_mid, v0[j : j + 1], v1[j : j + 1])
-        return carry
-
-    lax.fori_loop(0, last + 1, first, 0)
+    def row_of(p, i):
+        return frame[p, i + 4 : i + 5, :]
+
+    def advance(s, i):
+        new = step(states[s], i)
+        if s < STEPS - 1:
+            states[s + 1][i] = new
+        else:
+            field[8 * (i - HALO) : 8 * (i - HALO) + 8, :] = new[:, 0:cols]
+
+    for i in range(HALO, HALO + rows):
+        u_0[i] = jnp.broadcast_to(row_of(0, i), (8, cext))
+    for i in range(HALO + 1, HALO + rows - 1):
+        coefficients(i, ok_mid, row_of(1, i), row_of(2, i))
+    relay_wait(1)
     for s in range(STEPS):
-        def chunk(t, carry, s=s):
-            for j in range(8):
-                i = HALO + 8 * t + j
-                new = step(states[s], i)
-                if s < STEPS - 1:
-                    states[s + 1][i] = new
-                else:
-                    field[pl.ds(pl.multiple_of(64 * t + 8 * j, 8), 8), :] = new[:, 0:cols]
-            return carry
-        lax.fori_loop(0, last + 1, chunk, 0)
+        for i in range(HALO + s + 1, HALO + rows - s - 1):
+            advance(s, i)
 
     sens = sens_v[0]
     n_s = sens.shape[1]
@@ -296,16 +333,13 @@
 
     own = sensed(8, rows - 16, jnp.zeros((mem, n_s), jnp.float32))
 
-    for copy in halo_copies[0:4] + halo_copies[6:10]:
-        copy.wait_recv()
+    for k in (0, 1, 2, 3, 6, 7, 8, 9):
+        wait_halo(k)
     fill_extra(0, ok_top, corner_recv[2, 0], corner_recv[3, 0], last)
     fill_extra(last + 2, ok_bot, corner_recv[0, 1], corner_recv[1, 1], 0)
     for k in range(HALO):
         fill_kap(k, ok_top, corner_recv[2, 1], corner_recv[3, 1], per - HALO + k)
         fill_kap(HALO + rows + k, ok_bot, corner_recv[0, 0], corner_recv[1, 0], k)
-
-    def row_of(p, i):
-        return frame[p, i + 4 : i + 5, :]
 
     for k in range(HALO):
         u_0[k] = jnp.broadcast_to(row_of(0, k), (8, cext))
@@ -318,12 +352,8 @@
     for s in range(STEPS):
         for i in range(1 + s, HALO + 1 + s):
             j = 2 * HALO + rows - 1 - i
-            for q in (i, j):
-                new = step(states[s], q)
-                if s < STEPS - 1:
-                    states[s + 1][q] = new
-                else:
-                    field[8 * (q - HALO) : 8 * (q - HALO) + 8, :] = new[:, 0:cols]
+            advance(s, i)
+            advance(s, j)
     own = sensed(0, 8, own)
     own = sensed(rows - 8, 8, own)
     mine = pl.ds(pl.multiple_of(e * mem, mem), mem)
@@ -337,6 +367,7 @@
             copies.append(send(src, dst, ssem.at[d], rsem.at[d], device))
         return copies
 
+    relay_wait(2)
     copies = spread(preds.at[mine], preds.at[mine], pred_ssem, pred_rsem, ens_ids)
     for copy in copies:
         copy.wait_recv()
@@ -376,16 +407,36 @@
         copy.wait_recv()
     ybuf[x, y] = jnp.sum(zbuf[...], axis=0)
     copies = spread(ybuf.at[x, y], ybuf.at[x, y], y_ssem, y_rsem, y_ids)
+
+    def halves(index):
+        at = pl.ds(pl.multiple_of(index * mem * 8, mem * 8), mem * 8)
+        for t in range(rows // 8):
+            hi, lo = split_bf16(blocks[index, :, 8 * t : 8 * t + 8, :].reshape(mem * 8, cols))
+            th_hi[t, at, :] = hi
+            th_lo[t, at, :] = lo
+
+    other = x * 2 + 1 - core
+    for index in (e, near_l, near_r):
+        halves(index)
+    recv_half(4, other, 0)
+    recv_half(5, other, 1)
+    halves(other)
+    recv_half(6, far, 0)
+    send_half(far, 0, 12, to_o)
+    recv_half(7, far, 1)
+    send_half(far, 1, 13, to_o)
+    halves(far)
     for copy in copies:
         copy.wait_recv()
     gall[core] = jnp.sum(ybuf[...], axis=1)
     copies = [send(gall.at[core], gall.at[core], g_ssem.at[0], g_rsem.at[0], to_o)]
 
-    recv_half(6, far, 0)
-    send_half(far, 0, 12, to_o)
-    recv_half(7, far, 1)
-    send_half(far, 1, 13, to_o)
-
+    for h in range(2):
+        recv_half(8 + h, x_l * 2 + 1 - core, h)
+        recv_half(10 + h, x_r * 2 + 1 - core, h)
+        recv_half(12 + h, x_f * 2 + 1 - core, h)
+    for other in (x_l, x_r, x_f):
+        halves(other * 2 + 1 - core)
     for copy in copies:
         copy.wait_recv()
 
@@ -417,25 +468,18 @@
     b_hi, b_lo = split_bf16(big)
     b_both = jnp.concatenate([b_hi, b_lo], axis=0)
 
-    recv_half(4, x * 2 + 1 - core, 0)
-    recv_half(5, x * 2 + 1 - core, 1)
-    for h in range(2):
-        recv_half(8 + h, x_l * 2 + 1 - core, h)
-        recv_half(10 + h, x_r * 2 + 1 - core, h)
-        recv_half(12 + h, x_f * 2 + 1 - core, h)
-
     outs = []
     for t in range(rows // 8):
-        tile = blocks[:, :, 8 * t : 8 * t + 8, :].reshape(wide, cols)
-        t_hi, t_lo = split_bf16(tile)
-        two = dot32(b_both, t_hi)
-        new = two[: mem * 8] + (dot32(b_hi, t_lo) + two[mem * 8 :])
+        two = dot32(b_both, th_hi[t])
+        new = two[: mem * 8] + (dot32(b_hi, th_lo[t]) + two[mem * 8 :])
         result[:, 8 * t : 8 * t + 8, :] = new.reshape(mem, 8, cols)
         copy = pltpu.make_async_copy(
             result.at[:, pl.ds(8 * t, 8)], out.at[:, pl.ds(8 * t, 8)], out_sem.at[t]
         )
         copy.start()
         outs.append(copy)
+    for copy, there, _ in halo_copies:
+        pl.when(there)(copy.wait_send)
     for copy in sends:
         copy.wait_send()
     for copy in outs:
@@ -476,6 +520,8 @@
             pltpu.VMEM((n_z, mem, LANES), f32),
             pltpu.VMEM((n_e // 2, n_y, mem, LANES), f32),
             pltpu.VMEM((2, n_e // 2, mem, LANES), f32),
+            pltpu.VMEM((rows // 8, members * 8, cols), jnp.bfloat16),
+            pltpu.VMEM((rows // 8, members * 8, cols), jnp.bfloat16),
             pltpu.VMEM((mem, rows, cols), f32),
             DMA((6,)),
             DMA((10,)), DMA((10,)),
@@ -485,6 +531,7 @@
             DMA((1,)), DMA((1,)),
             DMA((14,)), DMA((14,)),
             DMA((rows // 8,)),
+            pltpu.SemaphoreType.REGULAR((3,)),
         ],
         compiler_params=pltpu.CompilerParams(
             collective_id=0, has_side_effects=True, vmem_limit_bytes=48 * 1024 * 1024

time: 51.6 us -> 48.5 us (0.940)
  Pallas kernels: 49.4 us -> 46.4 us
    pallas_call x1, Pallas kernels: 49.4 us -> 46.4 us  [shards(): pl.pallas_call(functools.partial(kernel, sizes), out_shape=(jax.ShapeDtyp...]
where the time goes in v3:
time: 48.5 us; the launch traced here: 48.4 us
  Pallas kernels  46.4 us (96%)
  local copies, waits for them, and re-layouts  1.39 us (3%)
  between operations  0.64 us (1%)
    pallas_call x1, Pallas kernels, shards(): pl.pallas_call(functools.partial(kernel, sizes), out_shape=(jax.ShapeDtyp...  46.4 us
    unnamed x2, local copies, waits for them, and re-layouts  1.39 us

profile of v3, /device:TPU:1, one launch (start us, length us, event | category | flops | bytes accessed | tf_op | source)
XLA Modules:
  0.0 48.4 jit_solution(254019940342925034)
XLA Ops:
  0.6 46.4 %shard_map.77 = (f32[8,64,256]{2,1,0:T(8,128)S(1)}, f32[8,1,1,256]{3,2,1,0:T(1,128)S(1)}) custom-call(f32[8,64,256]{2,1,0:T(8,128)} %theta.1, f32[64,256]{1,0:T(8,128)} %initial.1, f32[2,64,256]{2,1,0:T(8,128)} %velocity.1, s32[1,1,256]{2,1,0:T(1,128)} %sensors.1, f32[1,1,256]{2,1,0:T(1,128)} %target.1, f32[1,1,256]{2,1,0:T(1,128)} %noise.1), custom_call_target="tpu_custom_call" | custom-call | tf_op jit(solution)/shard_map/pallas_call | solution.py:498
  47.0 0.8 %copy.10 = f32[8,64,256]{2,1,0:T(8,128)} copy(f32[8,64,256]{2,1,0:T(8,128)S(1)} %get-tuple-element.4) | data formatting | bytes 1048576
  47.8 0.6 %copy.11 = f32[8,1,1,256]{3,2,1,0:T(1,128)} copy(f32[8,1,1,256]{3,2,1,0:T(1,128)S(1)} %get-tuple-element.5) | data formatting | bytes 16384

commit v4 on v3

--- a/solution.py
+++ b/solution.py
@@ -102,15 +102,9 @@
     ens_ids = [{"ens": (e + d) % n_e} for d in range(1, n_e)]
     z_ids = [{"row": yh * n_z + (z + d) % n_z} for d in range(1, n_z)]
     y_ids = []
-    for dy in sorted(range(n_y), key=lambda d: -min(d, n_y - d)):
-        for dx in sorted(range(n_x), key=lambda d: -min(d, n_x - d)):
-            if dx or dy:
-                other = (y + dy) % n_y
-                y_ids.append({
-                    "ens": (x + dx) % n_x * 2 + core,
-                    "row": other // n_c * n_z + z,
-                    "col": other % n_c,
-                })
+    for d in range(1, n_y):
+        other = (y + d) % n_y
+        y_ids.append({"row": other // n_c * n_z + z, "col": other % n_c})
 
     has_p, has_n, has_l, has_r = r > 0, r < n_r - 1, c > 0, c < n_c - 1
     halo_out = [
@@ -178,6 +172,11 @@
 
     def send_half(index, h, slot, device):
         return send(part(index, h), part(index, h), th_ssem.at[slot], th_rsem.at[slot], device)
+
+    send_half(e, 0, 0, to_r)
+    send_half(e, 1, 3, to_l)
+    for h in range(2):
+        send_half(e, h, 4 + h, to_o)
 
     def turned(t):
         tile = blocks[e, :, 8 * t : 8 * t + 8, :]
@@ -235,12 +234,6 @@
         part_k = pl.ds(0 if k < 2 else 1, 2)
         send_halo(6 + k, col_send.at[k % 2, part_k], corner_recv.at[k], 4 + k)
 
-    for h in range(2):
-        send_half(e, h, h, to_r)
-        send_half(e, 1 - h, 2 + 1 - h, to_l)
-    for h in range(2):
-        send_half(e, h, 4 + h, to_o)
-
     ci = lax.broadcasted_iota(jnp.int32, (8, cext), 1)
     c_lo = jnp.where(c < n_c - 1, cols + HALO, cols)
     c_hi = jnp.where(c > 0, cext - HALO, cext)
@@ -367,76 +360,74 @@
             copies.append(send(src, dst, ssem.at[d], rsem.at[d], device))
         return copies
 
+    copies = spread(preds.at[mine], preds.at[mine], pred_ssem, pred_rsem, ens_ids)
     relay_wait(2)
-    copies = spread(preds.at[mine], preds.at[mine], pred_ssem, pred_rsem, ens_ids)
+
+    def recv_half(slot, index, h):
+        remote(part(index, h), part(index, h), th_ssem.at[slot], th_rsem.at[slot], to_o).wait_recv()
+
+    near_l, near_r, far = x_l * 2 + core, x_r * 2 + core, x_f * 2 + core
+    other = x * 2 + 1 - core
+    recv_half(0, near_l, 0)
+    recv_half(3, near_r, 1)
     for copy in copies:
         copy.wait_recv()
 
+    send_half(e, 1, 1, to_r)
+    send_half(e, 0, 2, to_l)
+    send_half(near_l, 0, 6, to_r)
+    send_half(near_r, 1, 7, to_l)
+
     flat = preds[...]
-    mean = jnp.sum(flat, axis=0, keepdims=True) * (1.0 / (n_e * mem))
+    members = n_e * mem
+    hm, qm = members // 2, members // 4
+    mean = jnp.sum(flat, axis=0, keepdims=True) * (1.0 / members)
     inv_noise = 1.0 / noise_v[0]
-    weighted = (flat - mean) * inv_noise
-    miss = (targ_v[0] - mean) * inv_noise
-    members = n_e * mem
-    against = jnp.concatenate(
-        [weighted, miss, jnp.zeros((LANES - members - 1, n_s), jnp.float32)], axis=0
-    )
+    against = jnp.where(
+        lax.broadcasted_iota(jnp.int32, (members, n_s), 0) == members - 1,
+        targ_v[0] - mean, flat - mean,
+    ) * inv_noise
     gram = lax.dot_general(
-        preds[mine, :] - mean, against, (((1,), (1,)), ((), ())),
+        preds[pl.ds(pl.multiple_of(core * hm, hm), hm), :] - mean, against,
+        (((1,), (1,)), ((), ())),
         precision=lax.Precision.HIGHEST, preferred_element_type=jnp.float32,
     )
-
-    zbuf[z] = gram
+    zbuf[z] = jnp.concatenate([gram[:qm], gram[qm:]], axis=1)
     copies = spread(zbuf.at[z], zbuf.at[z], z_ssem, z_rsem, z_ids)
 
-    def recv_half(slot, index, h):
-        remote(part(index, h), part(index, h), th_ssem.at[slot], th_rsem.at[slot], to_o).wait_recv()
-
-    near_l, near_r, far = x_l * 2 + core, x_r * 2 + core, x_f * 2 + core
-    recv_half(0, near_l, 0)
-    send_half(near_l, 0, 6, to_r)
-    recv_half(3, near_r, 1)
-    send_half(near_r, 1, 7, to_l)
-    recv_half(1, near_l, 1)
-    recv_half(2, near_r, 0)
-    for h in range(2):
-        send_half(near_l, h, 8 + h, to_o)
-        send_half(near_r, h, 10 + h, to_o)
-
-    for copy in copies:
-        copy.wait_recv()
-    ybuf[x, y] = jnp.sum(zbuf[...], axis=0)
-    copies = spread(ybuf.at[x, y], ybuf.at[x, y], y_ssem, y_rsem, y_ids)
-
-    def halves(index):
-        at = pl.ds(pl.multiple_of(index * mem * 8, mem * 8), mem * 8)
+    def halves(index, slot):
+        at = slice(slot * mem * 8, (slot + 1) * mem * 8)
         for t in range(rows // 8):
             hi, lo = split_bf16(blocks[index, :, 8 * t : 8 * t + 8, :].reshape(mem * 8, cols))
             th_hi[t, at, :] = hi
             th_lo[t, at, :] = lo
 
-    other = x * 2 + 1 - core
-    for index in (e, near_l, near_r):
-        halves(index)
+    halves(e, 0)
     recv_half(4, other, 0)
     recv_half(5, other, 1)
-    halves(other)
-    recv_half(6, far, 0)
-    send_half(far, 0, 12, to_o)
-    recv_half(7, far, 1)
-    send_half(far, 1, 13, to_o)
-    halves(far)
+    halves(other, 1)
+    send_half(near_l, 0, 8, to_o)
+    send_half(near_r, 1, 11, to_o)
     for copy in copies:
         copy.wait_recv()
-    gall[core] = jnp.sum(ybuf[...], axis=1)
+
+    ybuf[y] = jnp.sum(zbuf[...], axis=0)
+    copies = spread(ybuf.at[y], ybuf.at[y], y_ssem, y_rsem, y_ids)
+    recv_half(1, near_l, 1)
+    recv_half(2, near_r, 0)
+    send_half(near_l, 1, 9, to_o)
+    send_half(near_r, 0, 10, to_o)
+    halves(near_l, 2)
+    halves(near_r, 4)
+    for copy in copies:
+        copy.wait_recv()
+    gall[core] = jnp.sum(ybuf[...], axis=0)
     copies = [send(gall.at[core], gall.at[core], g_ssem.at[0], g_rsem.at[0], to_o)]
-
     for h in range(2):
         recv_half(8 + h, x_l * 2 + 1 - core, h)
         recv_half(10 + h, x_r * 2 + 1 - core, h)
-        recv_half(12 + h, x_f * 2 + 1 - core, h)
-    for other in (x_l, x_r, x_f):
-        halves(other * 2 + 1 - core)
+    halves(x_l * 2 + 1 - core, 3)
+    halves(x_r * 2 + 1 - core, 5)
     for copy in copies:
         copy.wait_recv()
 
@@ -444,17 +435,27 @@
     acol = lax.broadcasted_iota(jnp.int32, (members, LANES), 1)
     first = members + 8
     unit = (arow == acol) | ((acol >= first) & (acol < first + mem) & (acol - first == arow - e * mem))
-    sums = jnp.concatenate([gall[i % 2, i // 2] for i in range(n_e)], axis=0)
+    quarters = [gall[q][:, w : w + members] for q in range(2) for w in (0, members)]
+    sums = jnp.concatenate(quarters, axis=0)
+    sums = jnp.concatenate([sums, jnp.zeros_like(sums)], axis=1)
+    others = jnp.sum(jnp.where(acol < members - 1, sums, 0.0), axis=1, keepdims=True)
+    sums = jnp.where(
+        acol == members - 1, -others,
+        jnp.where(acol == members, sums[:, members - 1 : members], sums),
+    )
     aug = sums * (1.0 / (members - 1)) + jnp.where(unit, 1.0, 0.0)
     aug = eliminate(aug, members, 8)
     weight = aug[:, first : first + mem] + aug[:, members : members + 1]
 
     wide = members * 8
-    pick = jnp.where(
-        lax.broadcasted_iota(jnp.int32, (members, wide), 0)
-        == lax.broadcasted_iota(jnp.int32, (members, wide), 1) // 8,
-        1.0, 0.0,
-    )
+    col_id = lax.broadcasted_iota(jnp.int32, (members, wide), 1)
+    slots = [e, other]
+    for chip in (x_l, x_r, x_f):
+        slots += [chip * 2 + core, chip * 2 + 1 - core]
+    k_of = (col_id // 8) % mem
+    for i, index in enumerate(slots):
+        k_of = jnp.where(col_id // (8 * mem) == i, k_of + index * mem, k_of)
+    pick = jnp.where(lax.broadcasted_iota(jnp.int32, (members, wide), 0) == k_of, 1.0, 0.0)
     spread_w = lax.dot_general(
         weight, pick, (((0,), (0,)), ((), ())),
         precision=lax.Precision.HIGHEST, preferred_element_type=jnp.float32,
@@ -468,11 +469,24 @@
     b_hi, b_lo = split_bf16(big)
     b_both = jnp.concatenate([b_hi, b_lo], axis=0)
 
+    def product(t, lo, hi):
+        two = dot32(b_both[:, lo:hi], th_hi[t, lo:hi, :])
+        return two[: mem * 8] + (dot32(b_hi[:, lo:hi], th_lo[t, lo:hi, :]) + two[mem * 8 :])
+
+    recv_half(6, far, 0)
+    send_half(far, 0, 12, to_o)
+    recv_half(7, far, 1)
+    send_half(far, 1, 13, to_o)
+    cut = wide - 2 * mem * 8
+    for t in range(rows // 8):
+        result[:, 8 * t : 8 * t + 8, :] = product(t, 0, cut).reshape(mem, 8, cols)
+    halves(far, 6)
+    recv_half(12, x_f * 2 + 1 - core, 0)
+    recv_half(13, x_f * 2 + 1 - core, 1)
+    halves(x_f * 2 + 1 - core, 7)
     outs = []
     for t in range(rows // 8):
-        two = dot32(b_both, th_hi[t])
-        new = two[: mem * 8] + (dot32(b_hi, th_lo[t]) + two[mem * 8 :])
-        result[:, 8 * t : 8 * t + 8, :] = new.reshape(mem, 8, cols)
+        result[:, 8 * t : 8 * t + 8, :] += product(t, cut, wide).reshape(mem, 8, cols)
         copy = pltpu.make_async_copy(
             result.at[:, pl.ds(8 * t, 8)], out.at[:, pl.ds(8 * t, 8)], out_sem.at[t]
         )
@@ -517,9 +531,9 @@
             *[pltpu.VMEM((rext, mem, cext), f32)] * 10,
             pltpu.VMEM((mem * rows, cols), f32),
             pltpu.VMEM((members, n_s), f32),
-            pltpu.VMEM((n_z, mem, LANES), f32),
-            pltpu.VMEM((n_e // 2, n_y, mem, LANES), f32),
-            pltpu.VMEM((2, n_e // 2, mem, LANES), f32),
+            pltpu.VMEM((n_z, members // 4, LANES), f32),
+            pltpu.VMEM((n_y, members // 4, LANES), f32),
+            pltpu.VMEM((2, members // 4, LANES), f32),
             pltpu.VMEM((rows // 8, members * 8, cols), jnp.bfloat16),
             pltpu.VMEM((rows // 8, members * 8, cols), jnp.bfloat16),
             pltpu.VMEM((mem, rows, cols), f32),
@@ -527,7 +541,7 @@
             DMA((10,)), DMA((10,)),
             DMA((n_e - 1,)), DMA((n_e - 1,)),
             DMA((n_z - 1,)), DMA((n_z - 1,)),
-            DMA((n_e // 2 * n_y - 1,)), DMA((n_e // 2 * n_y - 1,)),
+            DMA((n_y - 1,)), DMA((n_y - 1,)),
             DMA((1,)), DMA((1,)),
             DMA((14,)), DMA((14,)),
             DMA((rows // 8,)),

time: 48.5 us -> 45.8 us (0.944)
  Pallas kernels: 46.4 us -> 43.7 us
    pallas_call x1, Pallas kernels: 46.4 us -> 43.7 us  [shards(): pl.pallas_call(functools.partial(kernel, sizes), out_shape=(jax.ShapeDtyp...]
where the time goes in v4:
time: 45.8 us; the launch traced here: 45.7 us
  Pallas kernels  43.7 us (95%)
  local copies, waits for them, and re-layouts  1.39 us (3%)
  between operations  0.64 us (1%)
    pallas_call x1, Pallas kernels, shards(): pl.pallas_call(functools.partial(kernel, sizes), out_shape=(jax.ShapeDtyp...  43.7 us
    unnamed x2, local copies, waits for them, and re-layouts  1.39 us

profile of v4, /device:TPU:1, one launch (start us, length us, event | category | flops | bytes accessed | tf_op | source)
XLA Modules:
  0.0 45.7 jit_solution(4739350939687623110)
XLA Ops:
  0.6 43.7 %shard_map.77 = (f32[8,64,256]{2,1,0:T(8,128)S(1)}, f32[8,1,1,256]{3,2,1,0:T(1,128)S(1)}) custom-call(f32[8,64,256]{2,1,0:T(8,128)} %theta.1, f32[64,256]{1,0:T(8,128)} %initial.1, f32[2,64,256]{2,1,0:T(8,128)} %velocity.1, s32[1,1,256]{2,1,0:T(1,128)} %sensors.1, f32[1,1,256]{2,1,0:T(1,128)} %target.1, f32[1,1,256]{2,1,0:T(1,128)} %noise.1), custom_call_target="tpu_custom_call" | custom-call | tf_op jit(solution)/shard_map/pallas_call | solution.py:512
  44.3 0.8 %copy.10 = f32[8,64,256]{2,1,0:T(8,128)} copy(f32[8,64,256]{2,1,0:T(8,128)S(1)} %get-tuple-element.4) | data formatting | bytes 1048576
  45.1 0.6 %copy.11 = f32[8,1,1,256]{3,2,1,0:T(1,128)} copy(f32[8,1,1,256]{3,2,1,0:T(1,128)S(1)} %get-tuple-element.5) | data formatting | bytes 16384

commit v5 on v4

--- a/solution.py
+++ b/solution.py
@@ -131,10 +131,6 @@
         @pl.when(there)
         def _(device=device):
             pl.semaphore_signal(barrier, inc=1, device_id=device, device_id_type=MESH)
-    one = [jnp.where(v, 1, 0) for v in (has_p, has_n, has_l, has_r)]
-    n_halo = (1 + one[0] + one[1]) * (1 + one[2] + one[3]) - 1
-    pl.semaphore_wait(barrier, len(near_ids) + n_halo)
-
     def relay_signal(j):
         for device in near_ids:
             pl.semaphore_signal(
@@ -146,7 +142,6 @@
         if j < 2:
             relay_signal(j + 1)
 
-    relay_signal(0)
     sends = []
 
     def remote(src, dst, ssem, rsem, device):
@@ -173,11 +168,6 @@
     def send_half(index, h, slot, device):
         return send(part(index, h), part(index, h), th_ssem.at[slot], th_rsem.at[slot], device)
 
-    send_half(e, 0, 0, to_r)
-    send_half(e, 1, 3, to_l)
-    for h in range(2):
-        send_half(e, h, 4 + h, to_o)
-
     def turned(t):
         tile = blocks[e, :, 8 * t : 8 * t + 8, :]
         logk[HALO + 8 * t : HALO + 8 * t + 8] = jnp.swapaxes(tile, 0, 1)
@@ -203,10 +193,6 @@
     def edge_x(start):
         return extra.at[:, pl.ds(start, 8)]
 
-    send_halo(0, edge(HALO), edge(rows + HALO), 0)
-    send_halo(1, edge(rows), edge(0), 1)
-    send_halo(2, edge_x(8), edge_x(rows + 8), 0)
-    send_halo(3, edge_x(rows), edge_x(0), 1)
     for t in range(1, last):
         turned(t)
 
@@ -229,10 +215,24 @@
                 row = extra[p, 8 + 8 * t : 16 + 8 * t, low : low + LANES]
                 acc = jnp.where(slot_of == k, roll(row, HALO * k + off, 1), acc)
         col_send[side, 1] = acc
+    one = [jnp.where(v, 1, 0) for v in (has_p, has_n, has_l, has_r)]
+    n_halo = (1 + one[0] + one[1]) * (1 + one[2] + one[3]) - 1
+    pl.semaphore_wait(barrier, len(near_ids) + n_halo)
+
+    relay_signal(0)
+    send_halo(0, edge(HALO), edge(rows + HALO), 0)
+    send_halo(1, edge(rows), edge(0), 1)
+    send_halo(2, edge_x(8), edge_x(rows + 8), 0)
+    send_halo(3, edge_x(rows), edge_x(0), 1)
+    for side in range(2):
         send_halo(4 + side, col_send.at[side], col_recv.at[side], 2 + side)
     for k in range(4):
         part_k = pl.ds(0 if k < 2 else 1, 2)
         send_halo(6 + k, col_send.at[k % 2, part_k], corner_recv.at[k], 4 + k)
+    send_half(e, 0, 0, to_r)
+    send_half(e, 1, 3, to_l)
+    for h in range(2):
+        send_half(e, h, 4 + h, to_o)
 
     ci = lax.broadcasted_iota(jnp.int32, (8, cext), 1)
     c_lo = jnp.where(c < n_c - 1, cols + HALO, cols)
@@ -246,8 +246,10 @@
     def unpack(from_right, from_left, k):
         return jnp.where(near, roll(from_right, -HALO * k, 1), roll(from_left, -HALO - HALO * k, 1))
 
-    def fill_kap(i, ok, from_right, from_left, k):
+    def fill_centre(i, ok):
         kap[i, :, 0:cols] = jnp.where(ok[:, 0:cols], half_d * jnp.exp(logk[i]), 0.0)
+
+    def fill_outer(i, ok, from_right, from_left, k):
         outer = unpack(from_right, from_left, k)
         kap[i, :, cols:cext] = jnp.where(ok[:, cols:cext], half_d * jnp.exp(outer), 0.0)
 
@@ -279,6 +281,8 @@
 
     states = [u_0, u_1, u_2, u_3]
 
+    for i in range(rows):
+        fill_centre(HALO + i, ok_mid)
     relay_wait(0)
     wait_halo(4)
     wait_halo(5)
@@ -286,7 +290,7 @@
         fill_extra(t + 1, ok_mid, col_recv[0, 1], col_recv[1, 1], t)
     for i in range(rows):
         tile = 0 if i < per else 2
-        fill_kap(HALO + i, ok_mid, col_recv[0, tile], col_recv[1, tile], i % per)
+        fill_outer(HALO + i, ok_mid, col_recv[0, tile], col_recv[1, tile], i % per)
 
     def row_of(p, i):
         return frame[p, i + 4 : i + 5, :]
@@ -331,8 +335,10 @@
     fill_extra(0, ok_top, corner_recv[2, 0], corner_recv[3, 0], last)
     fill_extra(last + 2, ok_bot, corner_recv[0, 1], corner_recv[1, 1], 0)
     for k in range(HALO):
-        fill_kap(k, ok_top, corner_recv[2, 1], corner_recv[3, 1], per - HALO + k)
-        fill_kap(HALO + rows + k, ok_bot, corner_recv[0, 0], corner_recv[1, 0], k)
+        fill_centre(k, ok_top)
+        fill_outer(k, ok_top, corner_recv[2, 1], corner_recv[3, 1], per - HALO + k)
+        fill_centre(HALO + rows + k, ok_bot)
+        fill_outer(HALO + rows + k, ok_bot, corner_recv[0, 0], corner_recv[1, 0], k)
 
     for k in range(HALO):
         u_0[k] = jnp.broadcast_to(row_of(0, k), (8, cext))
@@ -368,15 +374,11 @@
 
     near_l, near_r, far = x_l * 2 + core, x_r * 2 + core, x_f * 2 + core
     other = x * 2 + 1 - core
-    recv_half(0, near_l, 0)
-    recv_half(3, near_r, 1)
     for copy in copies:
         copy.wait_recv()
 
     send_half(e, 1, 1, to_r)
     send_half(e, 0, 2, to_l)
-    send_half(near_l, 0, 6, to_r)
-    send_half(near_r, 1, 7, to_l)
 
     flat = preds[...]
     members = n_e * mem
@@ -406,11 +408,15 @@
     recv_half(4, other, 0)
     recv_half(5, other, 1)
     halves(other, 1)
+    recv_half(0, near_l, 0)
+    recv_half(3, near_r, 1)
     send_half(near_l, 0, 8, to_o)
     send_half(near_r, 1, 11, to_o)
     for copy in copies:
         copy.wait_recv()
 
+    send_half(near_l, 0, 6, to_r)
+    send_half(near_r, 1, 7, to_l)
     ybuf[y] = jnp.sum(zbuf[...], axis=0)
     copies = spread(ybuf.at[y], ybuf.at[y], y_ssem, y_rsem, y_ids)
     recv_half(1, near_l, 1)

time: 45.8 us -> 45.8 us (level)
  no operation moved by 1% of the time
where the time goes in v5:
time: 45.8 us; the launch traced here: 45.7 us
  Pallas kernels  43.7 us (95%)
  local copies, waits for them, and re-layouts  1.39 us (3%)
  between operations  0.64 us (1%)
    pallas_call x1, Pallas kernels, shards(): pl.pallas_call(functools.partial(kernel, sizes), out_shape=(jax.ShapeDtyp...  43.7 us
    unnamed x2, local copies, waits for them, and re-layouts  1.39 us

profile of v5, /device:TPU:1, one launch (start us, length us, event | category | flops | bytes accessed | tf_op | source)
XLA Modules:
  0.0 45.7 jit_solution(3561398707547876143)
XLA Ops:
  0.6 43.7 %shard_map.77 = (f32[8,64,256]{2,1,0:T(8,128)S(1)}, f32[8,1,1,256]{3,2,1,0:T(1,128)S(1)}) custom-call(f32[8,64,256]{2,1,0:T(8,128)} %theta.1, f32[64,256]{1,0:T(8,128)} %initial.1, f32[2,64,256]{2,1,0:T(8,128)} %velocity.1, s32[1,1,256]{2,1,0:T(1,128)} %sensors.1, f32[1,1,256]{2,1,0:T(1,128)} %target.1, f32[1,1,256]{2,1,0:T(1,128)} %noise.1), custom_call_target="tpu_custom_call" | custom-call | tf_op jit(solution)/shard_map/pallas_call | solution.py:518
  44.3 0.8 %copy.10 = f32[8,64,256]{2,1,0:T(8,128)} copy(f32[8,64,256]{2,1,0:T(8,128)S(1)} %get-tuple-element.4) | data formatting | bytes 1048576
  45.1 0.6 %copy.11 = f32[8,1,1,256]{3,2,1,0:T(1,128)} copy(f32[8,1,1,256]{3,2,1,0:T(1,128)S(1)} %get-tuple-element.5) | data formatting | bytes 16384

commit v6 on v5

--- a/solution.py
+++ b/solution.py
@@ -157,16 +157,34 @@
         sends.append(copy)
         return copy
 
+    one = [jnp.where(v, 1, 0) for v in (has_p, has_n, has_l, has_r)]
+    n_halo = (1 + one[0] + one[1]) * (1 + one[2] + one[3]) - 1
+    pl.semaphore_wait(barrier, len(near_ids) + n_halo)
+
+    relay_signal(0)
+
+    half = mem // 2
+
+    def part(index, h):
+        return blocks.at[index, pl.ds(h * half, half)]
+
+    def send_half(index, h, slot, device):
+        return send(part(index, h), part(index, h), th_ssem.at[slot], th_rsem.at[slot], device)
+
+    quarter = mem // 4
+
+    def send_first(start, count, slot, device):
+        here = pl.ds(start * quarter, count * quarter)
+        send(theta.at[here], blocks.at[e, here], th_ssem.at[slot], th_rsem.at[slot], device)
+
+    send_first(0, 2, 0, to_r)
+    send_first(2, 2, 3, to_l)
+    send_first(2, 1, 1, to_r)
+    send_first(1, 1, 2, to_l)
+    send_first(0, 4, 4, to_o)
+
     for copy in loads:
         copy.wait()
-
-    half = mem // 2
-
-    def part(index, h):
-        return blocks.at[index, pl.ds(h * half, half)]
-
-    def send_half(index, h, slot, device):
-        return send(part(index, h), part(index, h), th_ssem.at[slot], th_rsem.at[slot], device)
 
     def turned(t):
         tile = blocks[e, :, 8 * t : 8 * t + 8, :]
@@ -215,11 +233,6 @@
                 row = extra[p, 8 + 8 * t : 16 + 8 * t, low : low + LANES]
                 acc = jnp.where(slot_of == k, roll(row, HALO * k + off, 1), acc)
         col_send[side, 1] = acc
-    one = [jnp.where(v, 1, 0) for v in (has_p, has_n, has_l, has_r)]
-    n_halo = (1 + one[0] + one[1]) * (1 + one[2] + one[3]) - 1
-    pl.semaphore_wait(barrier, len(near_ids) + n_halo)
-
-    relay_signal(0)
     send_halo(0, edge(HALO), edge(rows + HALO), 0)
     send_halo(1, edge(rows), edge(0), 1)
     send_halo(2, edge_x(8), edge_x(rows + 8), 0)
@@ -229,11 +242,6 @@
     for k in range(4):
         part_k = pl.ds(0 if k < 2 else 1, 2)
         send_halo(6 + k, col_send.at[k % 2, part_k], corner_recv.at[k], 4 + k)
-    send_half(e, 0, 0, to_r)
-    send_half(e, 1, 3, to_l)
-    for h in range(2):
-        send_half(e, h, 4 + h, to_o)
-
     ci = lax.broadcasted_iota(jnp.int32, (8, cext), 1)
     c_lo = jnp.where(c < n_c - 1, cols + HALO, cols)
     c_hi = jnp.where(c > 0, cext - HALO, cext)
@@ -372,13 +380,21 @@
     def recv_half(slot, index, h):
         remote(part(index, h), part(index, h), th_ssem.at[slot], th_rsem.at[slot], to_o).wait_recv()
 
+    def recv_first(start, count, slot, index):
+        there = blocks.at[index, pl.ds(start * quarter, count * quarter)]
+        remote(there, there, th_ssem.at[slot], th_rsem.at[slot], to_o).wait_recv()
+
     near_l, near_r, far = x_l * 2 + core, x_r * 2 + core, x_f * 2 + core
     other = x * 2 + 1 - core
     for copy in copies:
         copy.wait_recv()
 
-    send_half(e, 1, 1, to_r)
-    send_half(e, 0, 2, to_l)
+    send_first(3, 1, 5, to_r)
+    send_first(0, 1, 14, to_l)
+    recv_half(0, near_l, 0)
+    send_half(near_l, 0, 6, to_r)
+    recv_half(3, near_r, 1)
+    send_half(near_r, 1, 7, to_l)
 
     flat = preds[...]
     members = n_e * mem
@@ -405,22 +421,19 @@
             th_lo[t, at, :] = lo
 
     halves(e, 0)
-    recv_half(4, other, 0)
-    recv_half(5, other, 1)
+    recv_first(0, 4, 4, other)
     halves(other, 1)
-    recv_half(0, near_l, 0)
-    recv_half(3, near_r, 1)
     send_half(near_l, 0, 8, to_o)
     send_half(near_r, 1, 11, to_o)
     for copy in copies:
         copy.wait_recv()
 
-    send_half(near_l, 0, 6, to_r)
-    send_half(near_r, 1, 7, to_l)
     ybuf[y] = jnp.sum(zbuf[...], axis=0)
     copies = spread(ybuf.at[y], ybuf.at[y], y_ssem, y_rsem, y_ids)
-    recv_half(1, near_l, 1)
-    recv_half(2, near_r, 0)
+    recv_first(2, 1, 1, near_l)
+    recv_first(3, 1, 5, near_l)
+    recv_first(1, 1, 2, near_r)
+    recv_first(0, 1, 14, near_r)
     send_half(near_l, 1, 9, to_o)
     send_half(near_r, 0, 10, to_o)
     halves(near_l, 2)
@@ -549,7 +562,7 @@
             DMA((n_z - 1,)), DMA((n_z - 1,)),
             DMA((n_y - 1,)), DMA((n_y - 1,)),
             DMA((1,)), DMA((1,)),
-            DMA((14,)), DMA((14,)),
+            DMA((15,)), DMA((15,)),
             DMA((rows // 8,)),
             pltpu.SemaphoreType.REGULAR((3,)),
         ],

time: 45.8 us -> 45.3 us (0.989)
  Pallas kernels: 43.7 us -> 43.1 us
    pallas_call x1, Pallas kernels: 43.7 us -> 43.1 us  [shards(): pl.pallas_call(functools.partial(kernel, sizes), out_shape=(jax.ShapeDtyp...]
where the time goes in v6:
time: 45.3 us; the launch traced here: 45.1 us
  Pallas kernels  43.1 us (95%)
  local copies, waits for them, and re-layouts  1.39 us (3%)
  between operations  0.64 us (1%)
    pallas_call x1, Pallas kernels, shards(): pl.pallas_call(functools.partial(kernel, sizes), out_shape=(jax.ShapeDtyp...  43.1 us
    unnamed x2, local copies, waits for them, and re-layouts  1.39 us

profile of v6, /device:TPU:1, one launch (start us, length us, event | category | flops | bytes accessed | tf_op | source)
XLA Modules:
  0.0 45.1 jit_solution(509170109658976742)
XLA Ops:
  0.6 43.1 %shard_map.77 = (f32[8,64,256]{2,1,0:T(8,128)S(1)}, f32[8,1,1,256]{3,2,1,0:T(1,128)S(1)}) custom-call(f32[8,64,256]{2,1,0:T(8,128)} %theta.1, f32[64,256]{1,0:T(8,128)} %initial.1, f32[2,64,256]{2,1,0:T(8,128)} %velocity.1, s32[1,1,256]{2,1,0:T(1,128)} %sensors.1, f32[1,1,256]{2,1,0:T(1,128)} %target.1, f32[1,1,256]{2,1,0:T(1,128)} %noise.1), custom_call_target="tpu_custom_call" | custom-call | tf_op jit(solution)/shard_map/pallas_call | solution.py:531
  43.8 0.8 %copy.10 = f32[8,64,256]{2,1,0:T(8,128)} copy(f32[8,64,256]{2,1,0:T(8,128)S(1)} %get-tuple-element.4) | data formatting | bytes 1048576
  44.6 0.6 %copy.11 = f32[8,1,1,256]{3,2,1,0:T(1,128)} copy(f32[8,1,1,256]{3,2,1,0:T(1,128)S(1)} %get-tuple-element.5) | data formatting | bytes 16384

commit v7 on v6

--- a/solution.py
+++ b/solution.py
@@ -391,10 +391,6 @@
 
     send_first(3, 1, 5, to_r)
     send_first(0, 1, 14, to_l)
-    recv_half(0, near_l, 0)
-    send_half(near_l, 0, 6, to_r)
-    recv_half(3, near_r, 1)
-    send_half(near_r, 1, 7, to_l)
 
     flat = preds[...]
     members = n_e * mem
@@ -412,6 +408,10 @@
     )
     zbuf[z] = jnp.concatenate([gram[:qm], gram[qm:]], axis=1)
     copies = spread(zbuf.at[z], zbuf.at[z], z_ssem, z_rsem, z_ids)
+    recv_half(0, near_l, 0)
+    send_half(near_l, 0, 6, to_r)
+    recv_half(3, near_r, 1)
+    send_half(near_r, 1, 7, to_l)
 
     def halves(index, slot):
         at = slice(slot * mem * 8, (slot + 1) * mem * 8)

time: 45.3 us -> 45.3 us (level)
  no operation moved by 1% of the time
where the time goes in v7:
time: 45.3 us; the launch traced here: 45.1 us
  Pallas kernels  43.1 us (95%)
  local copies, waits for them, and re-layouts  1.39 us (3%)
  between operations  0.64 us (1%)
    pallas_call x1, Pallas kernels, shards(): pl.pallas_call(functools.partial(kernel, sizes), out_shape=(jax.ShapeDtyp...  43.1 us
    unnamed x2, local copies, waits for them, and re-layouts  1.39 us

profile of v7, /device:TPU:1, one launch (start us, length us, event | category | flops | bytes accessed | tf_op | source)
XLA Modules:
  0.0 45.1 jit_solution(17541218038100570170)
XLA Ops:
  0.6 43.1 %shard_map.77 = (f32[8,64,256]{2,1,0:T(8,128)S(1)}, f32[8,1,1,256]{3,2,1,0:T(1,128)S(1)}) custom-call(f32[8,64,256]{2,1,0:T(8,128)} %theta.1, f32[64,256]{1,0:T(8,128)} %initial.1, f32[2,64,256]{2,1,0:T(8,128)} %velocity.1, s32[1,1,256]{2,1,0:T(1,128)} %sensors.1, f32[1,1,256]{2,1,0:T(1,128)} %target.1, f32[1,1,256]{2,1,0:T(1,128)} %noise.1), custom_call_target="tpu_custom_call" | custom-call | tf_op jit(solution)/shard_map/pallas_call | solution.py:531
  43.8 0.8 %copy.10 = f32[8,64,256]{2,1,0:T(8,128)} copy(f32[8,64,256]{2,1,0:T(8,128)S(1)} %get-tuple-element.4) | data formatting | bytes 1048576
  44.5 0.6 %copy.11 = f32[8,1,1,256]{3,2,1,0:T(1,128)} copy(f32[8,1,1,256]{3,2,1,0:T(1,128)S(1)} %get-tuple-element.5) | data formatting | bytes 16384
